TPU v7x, 32 devices: a whole 2x2x4 slice. The times are simulated.
32 devices in a mesh: dp: 4 (over z), zero: 8 (over y, x, core).
Axes of the slice: x: 2, y: 2, z: 4, core: 2. Of those that a mesh axis runs over, the one named last changes fastest.
Arguments:
- short_in: bfloat16 [32, 128, 768], P(('dp', 'zero')), may hold values from -6 to 6
- long_in: bfloat16 [32, 512, 768], P(('dp', 'zero')), may hold values from -6 to 6
- short_lengths: int32 [32], P(('dp', 'zero')), may hold values from 32 to 128, as said below
- long_lengths: int32 [32], P(('dp', 'zero')), may hold values from 128 to 512, as said below
- w_qkv: bfloat16 [2, 768, 2304], P(None, 'zero'), may hold values from -0.21875 to 0.21875
- q_bias: bfloat16 [2, 768], P(None, 'zero'), may hold values from -3 to 3
- v_bias: bfloat16 [2, 768], P(None, 'zero'), may hold values from -3 to 3
- w_out: bfloat16 [2, 768, 768], P(None, 'zero'), may hold values from -0.4375 to 0.4375
- out_bias: bfloat16 [2, 768], P(None, 'zero'), may hold values from -3 to 3
- norm1_gain: bfloat16 [2, 768], P(None, 'zero'), may hold values from 0.099609375 to 1.8984375
- norm1_bias: bfloat16 [2, 768], P(None, 'zero'), may hold values from -3 to 3
- w_gate_up: bfloat16 [2, 768, 6144], P(None, 'zero'), may hold values from -0.21875 to 0.21875
- w_down: bfloat16 [2, 3072, 768], P(None, 'zero'), may hold values from -0.15625 to 0.15625
- down_bias: bfloat16 [2, 768], P(None, 'zero'), may hold values from -3 to 3
- norm2_gain: bfloat16 [2, 768], P(None, 'zero'), may hold values from 0.099609375 to 1.8984375
- norm2_bias: bfloat16 [2, 768], P(None, 'zero'), may hold values from -3 to 3
- short_cot: bfloat16 [32, 128, 768], P(('dp', 'zero')), may hold values from -6 to 6
- long_cot: bfloat16 [32, 512, 768], P(('dp', 'zero')), may hold values from -6 to 6
Outputs:
- short_out: bfloat16 [32, 128, 768], P(('dp', 'zero'))
- long_out: bfloat16 [32, 512, 768], P(('dp', 'zero'))
- short_grad: float32 [32, 128, 768], P(('dp', 'zero'))
- long_grad: float32 [32, 512, 768], P(('dp', 'zero'))
- grad_w_qkv: float32 [2, 768, 2304], P(None, 'zero')
- grad_q_bias: float32 [2, 768], P(None, 'zero')
- grad_v_bias: float32 [2, 768], P(None, 'zero')
- grad_w_out: float32 [2, 768, 768], P(None, 'zero')
- grad_out_bias: float32 [2, 768], P(None, 'zero')
- grad_norm1_gain: float32 [2, 768], P(None, 'zero')
- grad_norm1_bias: float32 [2, 768], P(None, 'zero')
- grad_w_gate_up: float32 [2, 768, 6144], P(None, 'zero')
- grad_w_down: float32 [2, 3072, 768], P(None, 'zero')
- grad_down_bias: float32 [2, 768], P(None, 'zero')
- grad_norm2_gain: float32 [2, 768], P(None, 'zero')
- grad_norm2_bias: float32 [2, 768], P(None, 'zero')
Inputs may be any that keep to these rules, and one draw needn't show every extreme that they name: `short_lengths`: at least one short sequence has all 128 positions valid. `long_lengths`: at least one long sequence has all 512 positions valid.
All inputs are finite; a program needn't handle non-finite values.
Results may differ from a plain program's by a relative error of at most 0.03.
Values may be sent and summed in bfloat16 or wider, within the bound.
A program may use at most 256 MiB of HBM per device.

v0:
```python
import math

import jax
import jax.numpy as jnp
from jax import lax
from jax.sharding import PartitionSpec as P

HEADS = 12
LAYERS = 2


epsilon = 1e-05
masked_score = -1000000000.0


def head_slopes(head_count):
    power = 2 ** int(math.floor(math.log2(head_count)))
    first = [2.0 ** (-8.0 * (number + 1) / power) for number in range(power)]
    extra = [2.0 ** (-4.0 * (2 * number + 1) / power) for number in range(head_count - power)]
    return jnp.array(first + extra, jnp.float32)


def rows_product(left, right):
    return lax.dot_general(
        left, right, (((0,), (0,)), ((), ())), preferred_element_type=jnp.float32
    )


def times_transpose(left, right):
    return lax.dot_general(
        left, right, (((1,), (1,)), ((), ())), preferred_element_type=jnp.float32
    )


def normalize(summed, norm_gain, norm_bias):
    center = summed - jnp.mean(summed, axis=-1, keepdims=True)
    spread = jnp.mean(center * center, axis=-1, keepdims=True)
    inverse = lax.rsqrt(spread + epsilon)
    normed = center * inverse
    return (normed * norm_gain + norm_bias, normed, inverse)


def normalize_back(grad_out, normed, inverse, norm_gain):
    scaled = grad_out * norm_gain
    grad_in = inverse * (
        scaled
        - jnp.mean(scaled, axis=-1, keepdims=True)
        - normed * jnp.mean(scaled * normed, axis=-1, keepdims=True)
    )
    return (grad_in, jnp.sum(grad_out * normed, axis=0), jnp.sum(grad_out, axis=0))


def gated_gelu(gate_half, up_half):
    return jax.nn.gelu(gate_half, approximate=False) * up_half


def split_heads(matrix, seq_count, seq_len):
    head_width = matrix.shape[1] // HEADS
    return matrix.reshape(seq_count, seq_len, HEADS, head_width)


def layer_forward(inputs, lengths, weights):
    (
        w_qkv,
        q_bias,
        v_bias,
        w_out,
        out_bias,
        gain_one,
        bias_one,
        w_gate_up,
        w_down,
        down_bias,
        gain_two,
        bias_two,
    ) = weights
    seq_count, seq_len, model_width = inputs.shape
    hidden_width = w_down.shape[0]
    row_count = seq_count * seq_len
    score_scale = 1.0 / math.sqrt(model_width // HEADS)
    token_rows = inputs.reshape(row_count, model_width)
    projected = jnp.dot(token_rows, w_qkv, preferred_element_type=jnp.float32)
    queries = (projected[:, :model_width] + q_bias).astype(jnp.bfloat16)
    key_rows = projected[:, model_width : 2 * model_width].astype(jnp.bfloat16)
    values = (projected[:, 2 * model_width :] + v_bias).astype(jnp.bfloat16)
    query_heads = split_heads(queries, seq_count, seq_len)
    key_heads = split_heads(key_rows, seq_count, seq_len)
    value_heads = split_heads(values, seq_count, seq_len)
    positions = jnp.arange(seq_len, dtype=jnp.int32)
    distance = jnp.abs(positions[:, None] - positions[None, :]).astype(jnp.float32)
    slopes = head_slopes(HEADS)
    scores = (
        jnp.einsum("sqhd,skhd->shqk", query_heads, key_heads, preferred_element_type=jnp.float32)
        * score_scale
    )
    scores = scores - slopes[None, :, None, None] * distance[None, None]
    key_valid = positions[None, :] < lengths[:, None]
    scores = jnp.where(key_valid[:, None, None, :], scores, masked_score)
    row_max = jnp.max(scores, axis=-1, keepdims=True)
    exponent = jnp.exp(scores - row_max)
    attn_probs = exponent / jnp.sum(exponent, axis=-1, keepdims=True)
    probs_low = attn_probs.astype(jnp.bfloat16)
    mixed = jnp.einsum(
        "shqk,skhd->sqhd", probs_low, value_heads, preferred_element_type=jnp.float32
    )
    mixed = mixed.reshape(row_count, model_width).astype(jnp.bfloat16)
    branch = jnp.dot(mixed, w_out, preferred_element_type=jnp.float32) + out_bias
    hidden_full, normed_one, inverse_one = normalize(
        token_rows.astype(jnp.float32) + branch, gain_one, bias_one
    )
    hidden = hidden_full.astype(jnp.bfloat16)
    gate_up = jnp.dot(hidden, w_gate_up, preferred_element_type=jnp.float32)
    gate_half = gate_up[:, :hidden_width]
    up_half = gate_up[:, hidden_width:]
    inner_rows = gated_gelu(gate_half, up_half).astype(jnp.bfloat16)
    down_rows = jnp.dot(inner_rows, w_down, preferred_element_type=jnp.float32) + down_bias
    output_full, normed_two, inverse_two = normalize(
        hidden.astype(jnp.float32) + down_rows, gain_two, bias_two
    )
    valid = key_valid.reshape(row_count, 1).astype(jnp.float32)
    outputs = (output_full * valid).astype(jnp.bfloat16).reshape(seq_count, seq_len, model_width)
    saved = (
        token_rows,
        query_heads,
        key_heads,
        value_heads,
        attn_probs,
        probs_low,
        mixed,
        normed_one,
        inverse_one,
        hidden,
        gate_half,
        up_half,
        inner_rows,
        normed_two,
        inverse_two,
        valid,
    )
    return (outputs, saved)


def layer_backward(inputs, lengths, weights, grad_output):
    (
        w_qkv,
        q_bias,
        v_bias,
        w_out,
        out_bias,
        gain_one,
        bias_one,
        w_gate_up,
        w_down,
        down_bias,
        gain_two,
        bias_two,
    ) = weights
    outputs, saved = layer_forward(inputs, lengths, weights)
    (
        token_rows,
        query_heads,
        key_heads,
        value_heads,
        attn_probs,
        probs_low,
        mixed,
        normed_one,
        inverse_one,
        hidden,
        gate_half,
        up_half,
        inner_rows,
        normed_two,
        inverse_two,
        valid,
    ) = saved
    seq_count, seq_len, model_width = inputs.shape
    row_count = seq_count * seq_len
    score_scale = 1.0 / math.sqrt(model_width // HEADS)
    grad_rows = grad_output.reshape(row_count, model_width) * valid
    grad_sum_two, gaintwo_grad, biastwo_grad = normalize_back(
        grad_rows, normed_two, inverse_two, gain_two
    )
    grad_down = grad_sum_two.astype(jnp.bfloat16)
    bdown_grad = jnp.sum(grad_down, axis=0, dtype=jnp.float32)
    wdown_grad = rows_product(inner_rows, grad_down)
    grad_inner = times_transpose(grad_down, w_down)
    unused_value, gated_back = jax.vjp(gated_gelu, gate_half, up_half)
    grad_gate, grad_up = gated_back(grad_inner)
    grad_gate_up = jnp.concatenate([grad_gate, grad_up], axis=1).astype(jnp.bfloat16)
    gateup_grad = rows_product(hidden, grad_gate_up)
    grad_hidden = grad_sum_two + times_transpose(grad_gate_up, w_gate_up)
    grad_sum_one, gainone_grad, biasone_grad = normalize_back(
        grad_hidden, normed_one, inverse_one, gain_one
    )
    grad_branch = grad_sum_one.astype(jnp.bfloat16)
    bout_grad = jnp.sum(grad_branch, axis=0, dtype=jnp.float32)
    wout_grad = rows_product(mixed, grad_branch)
    grad_mixed = times_transpose(grad_branch, w_out).astype(jnp.bfloat16)
    mixed_heads = split_heads(grad_mixed, seq_count, seq_len)
    grad_probs = jnp.einsum(
        "sqhd,skhd->shqk", mixed_heads, value_heads, preferred_element_type=jnp.float32
    )
    row_dot = jnp.sum(attn_probs * grad_probs, axis=-1, keepdims=True)
    grad_scores = (attn_probs * (grad_probs - row_dot)).astype(jnp.bfloat16)
    grad_queries = jnp.einsum(
        "shqk,skhd->sqhd", grad_scores, key_heads, preferred_element_type=jnp.float32
    )
    grad_queries = (grad_queries * score_scale).astype(jnp.bfloat16).reshape(row_count, model_width)
    grad_keys = jnp.einsum(
        "shqk,sqhd->skhd", grad_scores, query_heads, preferred_element_type=jnp.float32
    )
    grad_keys = (grad_keys * score_scale).astype(jnp.bfloat16).reshape(row_count, model_width)
    grad_values = jnp.einsum(
        "shqk,sqhd->skhd", probs_low, mixed_heads, preferred_element_type=jnp.float32
    )
    grad_values = grad_values.astype(jnp.bfloat16).reshape(row_count, model_width)
    grad_projected = jnp.concatenate([grad_queries, grad_keys, grad_values], axis=1)
    qbias_grad = jnp.sum(grad_queries, axis=0, dtype=jnp.float32)
    vbias_grad = jnp.sum(grad_values, axis=0, dtype=jnp.float32)
    qkv_grad = rows_product(token_rows, grad_projected)
    grad_inputs = grad_sum_one + times_transpose(grad_projected, w_qkv)
    grads = (
        qkv_grad,
        qbias_grad,
        vbias_grad,
        wout_grad,
        bout_grad,
        gainone_grad,
        biasone_grad,
        gateup_grad,
        wdown_grad,
        bdown_grad,
        gaintwo_grad,
        biastwo_grad,
    )
    return (grad_inputs.reshape(seq_count, seq_len, model_width), grads)


def fetch_forward(params, layer_index):
    (
        w_qkv,
        q_bias,
        v_bias,
        w_out,
        out_bias,
        gain_one,
        bias_one,
        w_gate_up,
        w_down,
        down_bias,
        gain_two,
        bias_two,
    ) = tuple((param[layer_index] for param in params))
    return (
        lax.all_gather(w_qkv, "zero", axis=0, tiled=True),
        lax.all_gather(q_bias, "zero", axis=0, tiled=True),
        lax.all_gather(v_bias, "zero", axis=0, tiled=True),
        lax.all_gather(w_out, "zero", axis=0, tiled=True),
        lax.all_gather(out_bias, "zero", axis=0, tiled=True),
        lax.all_gather(gain_one, "zero", axis=0, tiled=True),
        lax.all_gather(bias_one, "zero", axis=0, tiled=True),
        lax.all_gather(w_gate_up, "zero", axis=0, tiled=True),
        lax.all_gather(w_down, "zero", axis=0, tiled=True),
        lax.all_gather(down_bias, "zero", axis=0, tiled=True),
        lax.all_gather(gain_two, "zero", axis=0, tiled=True),
        lax.all_gather(bias_two, "zero", axis=0, tiled=True),
    )


def fetch_again(params, layer_index):
    (
        w_qkv,
        q_bias,
        v_bias,
        w_out,
        out_bias,
        gain_one,
        bias_one,
        w_gate_up,
        w_down,
        down_bias,
        gain_two,
        bias_two,
    ) = tuple((param[layer_index] for param in params))
    return (
        lax.all_gather(w_qkv, "zero", axis=0, tiled=True),
        lax.all_gather(q_bias, "zero", axis=0, tiled=True),
        lax.all_gather(v_bias, "zero", axis=0, tiled=True),
        lax.all_gather(w_out, "zero", axis=0, tiled=True),
        lax.all_gather(out_bias, "zero", axis=0, tiled=True),
        lax.all_gather(gain_one, "zero", axis=0, tiled=True),
        lax.all_gather(bias_one, "zero", axis=0, tiled=True),
        lax.all_gather(w_gate_up, "zero", axis=0, tiled=True),
        lax.all_gather(w_down, "zero", axis=0, tiled=True),
        lax.all_gather(down_bias, "zero", axis=0, tiled=True),
        lax.all_gather(gain_two, "zero", axis=0, tiled=True),
        lax.all_gather(bias_two, "zero", axis=0, tiled=True),
    )


def reduce_grads(grads):
    (
        qkv_grad,
        qbias_grad,
        vbias_grad,
        wout_grad,
        bout_grad,
        gainone_grad,
        biasone_grad,
        gateup_grad,
        wdown_grad,
        bdown_grad,
        gaintwo_grad,
        biastwo_grad,
    ) = grads
    owned = (
        lax.psum_scatter(
            qkv_grad.astype(jnp.bfloat16), "zero", scatter_dimension=0, tiled=True
        ).astype(jnp.float32),
        lax.psum_scatter(
            qbias_grad.astype(jnp.bfloat16), "zero", scatter_dimension=0, tiled=True
        ).astype(jnp.float32),
        lax.psum_scatter(
            vbias_grad.astype(jnp.bfloat16), "zero", scatter_dimension=0, tiled=True
        ).astype(jnp.float32),
        lax.psum_scatter(
            wout_grad.astype(jnp.bfloat16), "zero", scatter_dimension=0, tiled=True
        ).astype(jnp.float32),
        lax.psum_scatter(
            bout_grad.astype(jnp.bfloat16), "zero", scatter_dimension=0, tiled=True
        ).astype(jnp.float32),
        lax.psum_scatter(
            gainone_grad.astype(jnp.bfloat16), "zero", scatter_dimension=0, tiled=True
        ).astype(jnp.float32),
        lax.psum_scatter(
            biasone_grad.astype(jnp.bfloat16), "zero", scatter_dimension=0, tiled=True
        ).astype(jnp.float32),
        lax.psum_scatter(
            gateup_grad.astype(jnp.bfloat16), "zero", scatter_dimension=0, tiled=True
        ).astype(jnp.float32),
        lax.psum_scatter(
            wdown_grad.astype(jnp.bfloat16), "zero", scatter_dimension=0, tiled=True
        ).astype(jnp.float32),
        lax.psum_scatter(
            bdown_grad.astype(jnp.bfloat16), "zero", scatter_dimension=0, tiled=True
        ).astype(jnp.float32),
        lax.psum_scatter(
            gaintwo_grad.astype(jnp.bfloat16), "zero", scatter_dimension=0, tiled=True
        ).astype(jnp.float32),
        lax.psum_scatter(
            biastwo_grad.astype(jnp.bfloat16), "zero", scatter_dimension=0, tiled=True
        ).astype(jnp.float32),
    )
    (
        qkv_owned,
        qbias_owned,
        vbias_owned,
        wout_owned,
        bout_owned,
        gainone_owned,
        biasone_owned,
        gateup_owned,
        wdown_owned,
        bdown_owned,
        gaintwo_owned,
        biastwo_owned,
    ) = owned
    return (
        lax.psum(qkv_owned.astype(jnp.bfloat16), "dp").astype(jnp.float32),
        lax.psum(qbias_owned.astype(jnp.bfloat16), "dp").astype(jnp.float32),
        lax.psum(vbias_owned.astype(jnp.bfloat16), "dp").astype(jnp.float32),
        lax.psum(wout_owned.astype(jnp.bfloat16), "dp").astype(jnp.float32),
        lax.psum(bout_owned.astype(jnp.bfloat16), "dp").astype(jnp.float32),
        lax.psum(gainone_owned.astype(jnp.bfloat16), "dp").astype(jnp.float32),
        lax.psum(biasone_owned.astype(jnp.bfloat16), "dp").astype(jnp.float32),
        lax.psum(gateup_owned.astype(jnp.bfloat16), "dp").astype(jnp.float32),
        lax.psum(wdown_owned.astype(jnp.bfloat16), "dp").astype(jnp.float32),
        lax.psum(bdown_owned.astype(jnp.bfloat16), "dp").astype(jnp.float32),
        lax.psum(gaintwo_owned.astype(jnp.bfloat16), "dp").astype(jnp.float32),
        lax.psum(biastwo_owned.astype(jnp.bfloat16), "dp").astype(jnp.float32),
    )


def per_device(
    short_in,
    long_in,
    short_lengths,
    long_lengths,
    w_qkv,
    q_bias,
    v_bias,
    w_out,
    out_bias,
    norm1_gain,
    norm1_bias,
    w_gate_up,
    w_down,
    down_bias,
    norm2_gain,
    norm2_bias,
    short_cot,
    long_cot,
):
    params = (
        w_qkv,
        q_bias,
        v_bias,
        w_out,
        out_bias,
        norm1_gain,
        norm1_bias,
        w_gate_up,
        w_down,
        down_bias,
        norm2_gain,
        norm2_bias,
    )
    kept_weights = []
    short_acts = [short_in]
    long_acts = [long_in]
    for layer_index in range(LAYERS):
        weights = fetch_forward(params, layer_index)
        kept_weights.append(weights)
        short_next, short_saved = layer_forward(short_acts[-1], short_lengths, weights)
        long_next, long_saved = layer_forward(long_acts[-1], long_lengths, weights)
        short_acts.append(short_next)
        long_acts.append(long_next)
    short_grad = short_cot.astype(jnp.float32)
    long_grad = long_cot.astype(jnp.float32)
    reduced = [None] * LAYERS
    for layer_index in reversed(range(LAYERS)):
        weights = fetch_again(params, layer_index)
        short_grad, short_terms = layer_backward(
            short_acts[layer_index], short_lengths, weights, short_grad
        )
        long_grad, long_terms = layer_backward(
            long_acts[layer_index], long_lengths, weights, long_grad
        )
        summed_terms = jax.tree.map(jnp.add, short_terms, long_terms)
        reduced[layer_index] = reduce_grads(summed_terms)
    stacked = [
        jnp.stack([reduced[layer_index][member] for layer_index in range(LAYERS)])
        for member in range(len(params))
    ]
    return (short_acts[-1], long_acts[-1], short_grad, long_grad) + tuple(stacked)


def solution(mesh):
    placed = (
        P(("dp", "zero"), None, None),
        P(("dp", "zero"), None, None),
        P(("dp", "zero")),
        P(("dp", "zero")),
        P(None, "zero", None),
        P(None, "zero"),
        P(None, "zero"),
        P(None, "zero", None),
        P(None, "zero"),
        P(None, "zero"),
        P(None, "zero"),
        P(None, "zero", None),
        P(None, "zero", None),
        P(None, "zero"),
        P(None, "zero"),
        P(None, "zero"),
        P(("dp", "zero"), None, None),
        P(("dp", "zero"), None, None),
    )
    return jax.shard_map(
        per_device,
        mesh=mesh,
        in_specs=placed,
        out_specs=(
            P(("dp", "zero"), None, None),
            P(("dp", "zero"), None, None),
            P(("dp", "zero"), None, None),
            P(("dp", "zero"), None, None),
            P(None, "zero", None),
            P(None, "zero"),
            P(None, "zero"),
            P(None, "zero", None),
            P(None, "zero"),
            P(None, "zero"),
            P(None, "zero"),
            P(None, "zero", None),
            P(None, "zero", None),
            P(None, "zero"),
            P(None, "zero"),
            P(None, "zero"),
        ),
        check_vma=False,
    )
```

profile of v0, /device:TPU:0, one launch (start us, length us, event | category | flops | bytes accessed | tf_op | source)
XLA Modules:
  0.0 1216.8 jit_solution(5822160815492887746)
XLA Ops:
  24.0 26.7 %all-reduce.33 = (bf16[768]{0:T(1024)(128)(2,1)S(1)}, bf16[768]{0:T(1024)(128)(2,1)S(1)}, bf16[768]{0:T(1024)(128)(2,1)S(1)}, bf16[768]{0:T(1024)(128)(2,1)S(1)}...) all-reduce(bf16[768]{0:T(1024)(128)(2,1)S(1)} %dynamic-update-slice, ...), channel_id=3, replica_groups=mesh['dp'=4,'zero'=8] {'zero'}, use_global_device_ids=true, to_apply=%add | all-reduce | flops 11520 | bytes 46080
  69.5 9.8 fusion.306
  97.3 37.4 %all-gather.37.cloned.1.call-done = bf16[1,768,6144]{2,1,0:T(8,128)(2,1)} async-done(((bf16[1,96,6144]{2,1,0:T(8,128)(2,1)}), bf16[1,768,6144]{2,1,0:T(8,128)(2,1)}) %all-gather.37.cloned.1.call-update) | async-done | bytes 9437200 | tf_op jit(solution)/shard_map/all_gather | solution.py:263
  147.4 14.7 %multiply_convert_fusion.5 = (bf16[512,3072]{1,0:T(8,128)(2,1)}, f32[512,3072]{1,0:T(8,128)}) fusion(f32[512,6144]{1,0:T(8,128)S(1)} %fusion.18), kind=kLoop, calls=%fused_computation.62 | loop fusion | flops 103809024 | bytes 22020096 | tf_op jit(solution)/shard_map/convert_element_type | solution.py:115
  162.1 13.9 %all-gather.39.cloned.1.call-done = bf16[1,3072,768]{2,1,0:T(8,128)(2,1)} async-done(((bf16[1,384,768]{2,1,0:T(8,128)(2,1)}), bf16[1,3072,768]{2,1,0:T(8,128)(2,1)}) %all-gather.39.cloned.1.call-update) | async-done | bytes 4718608 | tf_op jit(solution)/shard_map/all_gather | solution.py:264
  182.4 29.3 %all-gather.41.cloned.1.call-done = bf16[1,768,2304]{2,1,0:T(8,128)(2,1)} async-done(((bf16[1,96,2304]{2,1,0:T(8,128)(2,1)}), bf16[1,768,2304]{2,1,0:T(8,128)(2,1)}) %all-gather.41.cloned.1.call-update) | async-done | bytes 3538960 | tf_op jit(solution)/shard_map/all_gather | solution.py:256
  219.6 9.4 fusion.309
  240.8 58.1 %all-gather.45.cloned.1.call-done = bf16[1,768,6144]{2,1,0:T(8,128)(2,1)} async-done(((bf16[1,96,6144]{2,1,0:T(8,128)(2,1)}), bf16[1,768,6144]{2,1,0:T(8,128)(2,1)}) %all-gather.45.cloned.1.call-update) | async-done | bytes 9437200 | tf_op jit(solution)/shard_map/all_gather | solution.py:263
  311.5 14.7 %multiply_convert_fusion.4 = (bf16[512,3072]{1,0:T(8,128)(2,1)}, f32[512,3072]{1,0:T(8,128)}) fusion(f32[512,6144]{1,0:T(8,128)S(1)} %fusion.10), kind=kLoop, calls=%fused_computation.48 | loop fusion | flops 103809024 | bytes 22020096 | tf_op jit(solution)/shard_map/convert_element_type | solution.py:115
  326.2 14.1 %all-gather.47.cloned.1.call-done = bf16[1,3072,768]{2,1,0:T(8,128)(2,1)} async-done(((bf16[1,384,768]{2,1,0:T(8,128)(2,1)}), bf16[1,3072,768]{2,1,0:T(8,128)(2,1)}) %all-gather.47.cloned.1.call-update) | async-done | bytes 4718608 | tf_op jit(solution)/shard_map/all_gather | solution.py:264
  352.0 10.4 add_convert_fusion.7
  362.4 12.2 %multiply_reduce_fusion.3 = (f32[768]{0:T(1024)}, f32[512]{0:T(512)S(1)}, f32[512]{0:T(512)S(1)}, f32[768]{0:T(1024)}, f32[512,768]{1,0:T(8,128)S(1)}) fusion(f32[512,768]{1,0:T(8,128)S(1)} %get-tuple-element.244, f32[512]{0:T(512)S(1)} %add_rsqrt_fusion.1, f32[512]{0:T(512)S(1)} %broadcast_multiply_fusion.9, f32[768]{0:T(1024)S(1)} %convert_element_type.1023, ...), kind=kOutput, calls=%fused_computation.170 | convolution fusion | flops 4848350208 | bytes 20464640 | tf_op jit(solution)/shard_map/dot_general | solution.py:30
  378.8 10.2 multiply_reduce_fusion.1
  389.0 8.3 convert_reduce_fusion.4
  466.0 10.4 add_convert_fusion.6
  476.4 12.1 multiply_reduce_fusion.4
  494.9 8.4 convert_reduce_fusion.5
  503.3 9.0 multiply_reduce_fusion
  591.2 12.1 fusion.71
  603.3 10.5 add_convert_fusion.1
  615.4 12.6 %fusion.72 = f32[768,6144]{1,0:T(8,128)} fusion(bf16[512,3072]{1,0:T(8,128)(2,1)} %get-tuple-element.179, bf16[512,3072]{1,0:T(8,128)(2,1)} %get-tuple-element.178, f32[512,768]{1,0:T(8,128)S(1)} %copy-done.11, f32[768]{0:T(1024)S(1)} %copy-done.102, f32[768]{0:T(1024)S(1)} %convert_element_type.1023, f32[512]{0:T(512)S(1)} %copy-done.130, ...), kind=kOutput, calls=%fused_computation.110 | convolution fusion | flops 4846387200 | bytes 26748928 | tf_op jit(solution)/shard_map/dot_general | solution.py:24
  628.0 11.0 add_convert_fusion
  643.0 12.7 %reduce-scatter.27.cloned.1.call-done = bf16[96,2304]{1,0:T(8,128)(2,1)} async-done(((bf16[768,2304]{1,0:T(8,128)(2,1)}), bf16[96,2304]{1,0:T(8,128)(2,1)}) %reduce-scatter.27.cloned.1.call-update) | async-done | bytes 442384
  657.7 38.5 %reduce-scatter.13.cloned.1.call-done = bf16[96,768]{1,0:T(8,128)(2,1)} async-done(((bf16[768,768]{1,0:T(8,128)(2,1)}), bf16[96,768]{1,0:T(8,128)(2,1)}) %reduce-scatter.13.cloned.1.call-update) | async-done | bytes 147472 | tf_op jit(solution)/shard_map/reduce_scatter | solution.py:327
  696.3 40.8 %reduce-scatter.15.cloned.1.call-done = bf16[96,768]{1,0:T(8,128)(2,1)} async-done(((bf16[768,768]{1,0:T(8,128)(2,1)}), bf16[96,768]{1,0:T(8,128)(2,1)}) %reduce-scatter.15.cloned.1.call-update) | async-done | bytes 147472 | tf_op jit(solution)/shard_map/reduce_scatter | solution.py:327
  737.1 57.3 %reduce-scatter.21.cloned.1.call-done = bf16[384,768]{1,0:T(8,128)(2,1)} async-done(((bf16[3072,768]{1,0:T(8,128)(2,1)}), bf16[384,768]{1,0:T(8,128)(2,1)}) %reduce-scatter.21.cloned.1.call-update) | async-done | bytes 589840 | tf_op jit(solution)/shard_map/reduce_scatter | solution.py:342
  794.4 58.2 %reduce-scatter.23.cloned.1.call-done = bf16[384,768]{1,0:T(8,128)(2,1)} async-done(((bf16[3072,768]{1,0:T(8,128)(2,1)}), bf16[384,768]{1,0:T(8,128)(2,1)}) %reduce-scatter.23.cloned.1.call-update) | async-done | bytes 589840 | tf_op jit(solution)/shard_map/reduce_scatter | solution.py:342
  852.6 79.9 %reduce-scatter.17.cloned.1.call-done = bf16[96,6144]{1,0:T(8,128)(2,1)} async-done(((bf16[768,6144]{1,0:T(8,128)(2,1)}), bf16[96,6144]{1,0:T(8,128)(2,1)}) %reduce-scatter.17.cloned.1.call-update) | async-done | bytes 1179664 | tf_op jit(solution)/shard_map/reduce_scatter | solution.py:339
  932.5 79.9 %reduce-scatter.19.cloned.1.call-done = bf16[96,6144]{1,0:T(8,128)(2,1)} async-done(((bf16[768,6144]{1,0:T(8,128)(2,1)}), bf16[96,6144]{1,0:T(8,128)(2,1)}) %reduce-scatter.19.cloned.1.call-update) | async-done | bytes 1179664 | tf_op jit(solution)/shard_map/reduce_scatter | solution.py:339
  1013.5 24.4 %all-reduce.32 = (bf16[768]{0:T(1024)(128)(2,1)S(1)}, bf16[768]{0:T(1024)(128)(2,1)S(1)}, bf16[768]{0:T(1024)(128)(2,1)S(1)}, bf16[768]{0:T(1024)(128)(2,1)S(1)}...) all-reduce(bf16[768]{0:T(1024)(128)(2,1)S(1)} %dynamic-update-slice, ...), channel_id=25, replica_groups=mesh['dp'=4,'zero'=8] {'zero'}, use_global_device_ids=true, to_apply=%add.15 | all-reduce | flops 13056 | bytes 52224
  1039.1 12.7 %all-reduce.34 = (bf16[1,96]{1,0:T(2,128)(2,1)S(1)}, bf16[1,96]{1,0:T(2,128)(2,1)S(1)}, bf16[1,96]{1,0:T(2,128)(2,1)S(1)}, bf16[1,96]{1,0:T(2,128)(2,1)S(1)}, bf...) all-reduce(bf16[1,96]{1,0:T(2,128)(2,1)S(1)} %dynamic-slice_bitcast, ...), channel_id=1, replica_groups=mesh['dp'=4,'zero'=8] {'dp'}, use_global_device_ids=true, to_apply=%region_79.80 | all-reduce | flops 1536 | bytes 6144 | tf_op jit(solution)/shard_map/psum | solution.py:371
  1067.1 133.7 %all-reduce.38.cloned.1.call-done = (bf16[1,96,2304]{1,2,0:T(8,128)(2,1)}, bf16[1,96,2304]{1,2,0:T(8,128)(2,1)}, bf16[1,96,768]{2,1,0:T(8,128)(2,1)}, bf16[1,96,...) async-done(((bf16[1,96,2304]{1,2,0:T(8,128)(2,1)}, ...) | async-done | bytes 4718608 | tf_op jit(solution)/shard_map/psum | solution.py:370
  (819 shorter events, 303.3 us)
Async XLA Ops:
  7.2 52.3 %all-gather.33.cloned.1.call-start = ((), (), s32[]{:S(2)}) async-start(), calls=%async_computation.14 | async-start | bytes 3981312 | tf_op jit(solution)/shard_map/all_gather | solution.py:256
  9.5 76.3 %all-gather.35.cloned.1.call-start = ((), (), s32[]{:S(2)}) async-start(), calls=%async_computation.15 | async-start | bytes 1327104 | tf_op jit(solution)/shard_map/all_gather | solution.py:259
  10.4 124.4 %all-gather.37.cloned.1.call-start = ((), (), s32[]{:S(2)}) async-start(), calls=%async_computation.16 | async-start | bytes 10616832 | tf_op jit(solution)/shard_map/all_gather | solution.py:263
  12.0 164.0 %all-gather.39.cloned.1.call-start = ((), (), s32[]{:S(2)}) async-start(), calls=%async_computation.17 | async-start | bytes 5308416 | tf_op jit(solution)/shard_map/all_gather | solution.py:264
  14.4 197.4 %all-gather.41.cloned.1.call-start = ((), (), s32[]{:S(2)}) async-start(), calls=%async_computation.18 | async-start | bytes 3981312 | tf_op jit(solution)/shard_map/all_gather | solution.py:256
  15.1 222.5 %all-gather.43.cloned.1.call-start = ((), (), s32[]{:S(2)}) async-start(), calls=%async_computation.19 | async-start | bytes 1327104 | tf_op jit(solution)/shard_map/all_gather | solution.py:259
  15.6 283.2 %all-gather.45.cloned.1.call-start = ((), (), s32[]{:S(2)}) async-start(), calls=%async_computation.20 | async-start | bytes 10616832 | tf_op jit(solution)/shard_map/all_gather | solution.py:263
  16.4 323.9 %all-gather.47.cloned.1.call-start = ((), (), s32[]{:S(2)}) async-start(), calls=%async_computation.21 | async-start | bytes 5308416 | tf_op jit(solution)/shard_map/all_gather | solution.py:264
  17.1 623.8 %reduce-scatter.25.cloned.1.call-start = ((), (), s32[]{:S(2)}) async-start(), calls=%async_computation.22 | async-start | bytes 3981312
  52.5 363.3 %copy-start.103 = (f32[768]{0:T(1024)}, f32[768]{0:T(1024)S(1)}, u32[]{:S(2)}) copy-start(f32[768]{0:T(1024)S(1)} %convert_element_type.1016) | copy-start | bytes 9220
  56.6 377.6 %copy-start.101 = (f32[768]{0:T(1024)}, f32[768]{0:T(1024)S(1)}, u32[]{:S(2)}) copy-start(f32[768]{0:T(1024)S(1)} %convert_element_type.1024) | copy-start | bytes 9220
  88.5 87.5 %copy-start.8 = (f32[512,768]{1,0:T(8,128)}, f32[512,768]{1,0:T(8,128)S(1)}, u32[]{:S(2)}) copy-start(f32[512,768]{1,0:T(8,128)S(1)} %get-tuple-element.238) | copy-start | bytes 4718596
  94.7 48.0 %copy-start.62 = (bf16[12,64,128]{2,1,0:T(8,128)(2,1)}, bf16[12,64,128]{2,1,0:T(8,128)(2,1)S(1)}, u32[]{:S(2)}) copy-start(bf16[12,64,128]{2,1,0:T(8,128)(2,1)S(1)} %convolution_convert_fusion.5) | copy-start | bytes 589828
  95.9 46.8 %copy-start.153 = (f32[128]{0:T(128)}, f32[128]{0:T(128)S(1)}, u32[]{:S(2)}) copy-start(f32[128]{0:T(128)S(1)} %broadcast_multiply_fusion.23) | copy-start | bytes 1540
  182.1 55.5 %copy-start.159 = (f32[512]{0:T(512)}, f32[512]{0:T(512)S(1)}, u32[]{:S(2)}) copy-start(f32[512]{0:T(512)S(1)} %broadcast_multiply_fusion.10) | copy-start | bytes 6148
  182.4 55.2 %copy-start.193 = (f32[512]{0:T(512)}, f32[512]{0:T(512)S(1)}, u32[]{:S(2)}) copy-start(f32[512]{0:T(512)S(1)} %add_rsqrt_fusion.2) | copy-start | bytes 6148
  240.4 134.1 %copy-start.10 = (f32[512,768]{1,0:T(8,128)}, f32[512,768]{1,0:T(8,128)S(1)}, u32[]{:S(2)}) copy-start(f32[512,768]{1,0:T(8,128)S(1)} %get-tuple-element.244) | copy-start | bytes 4718596
  240.4 134.1 %copy-start.119 = (f32[512]{0:T(512)}, f32[512]{0:T(512)S(1)}, u32[]{:S(2)}) copy-start(f32[512]{0:T(512)S(1)} %broadcast_multiply_fusion.9) | copy-start | bytes 6148
  240.8 133.8 %copy-start.129 = (f32[512]{0:T(512)}, f32[512]{0:T(512)S(1)}, u32[]{:S(2)}) copy-start(f32[512]{0:T(512)S(1)} %add_rsqrt_fusion.1) | copy-start | bytes 6148
  447.5 77.4 %copy-start.36 = (f32[128,768]{1,0:T(8,128)}, f32[128,768]{1,0:T(8,128)S(1)}, u32[]{:S(2)}) copy-start(f32[128,768]{1,0:T(8,128)S(1)} %get-tuple-element.167) | copy-start | bytes 1179652
  556.0 99.7 %reduce-scatter.27.cloned.1.call-start = ((), (), s32[]{:S(2)}) async-start(), calls=%async_computation.23 | async-start | bytes 3981312
  564.0 132.2 %reduce-scatter.13.cloned.1.call-start = ((), (), s32[]{:S(2)}) async-start(), calls=%async_computation.8 | async-start | bytes 1327104 | tf_op jit(solution)/shard_map/reduce_scatter | solution.py:327
  568.3 168.8 %reduce-scatter.15.cloned.1.call-start = ((), (), s32[]{:S(2)}) async-start(), calls=%async_computation.9 | async-start | bytes 1327104 | tf_op jit(solution)/shard_map/reduce_scatter | solution.py:327
  572.4 222.0 %reduce-scatter.21.cloned.1.call-start = ((), (), s32[]{:S(2)}) async-start(), calls=%async_computation.12 | async-start | bytes 5308416 | tf_op jit(solution)/shard_map/reduce_scatter | solution.py:342
  581.3 271.3 %reduce-scatter.23.cloned.1.call-start = ((), (), s32[]{:S(2)}) async-start(), calls=%async_computation.13 | async-start | bytes 5308416 | tf_op jit(solution)/shard_map/reduce_scatter | solution.py:342
  590.5 342.0 %reduce-scatter.17.cloned.1.call-start = ((), (), s32[]{:S(2)}) async-start(), calls=%async_computation.10 | async-start | bytes 10616832 | tf_op jit(solution)/shard_map/reduce_scatter | solution.py:339
  613.9 398.5 %reduce-scatter.19.cloned.1.call-start = ((), (), s32[]{:S(2)}) async-start(), calls=%async_computation.11 | async-start | bytes 10616832 | tf_op jit(solution)/shard_map/reduce_scatter | solution.py:339
  639.2 561.5 %all-reduce.38.cloned.1.call-start = ((), (), s32[]{:S(2)}) async-start(), calls=%async_computation.24 | async-start | bytes 10027008 | tf_op jit(solution)/shard_map/psum | solution.py:370
  1012.5 44.8 %copy-start.1 = (f32[512,768]{1,0:T(8,128)S(1)}, f32[512,768]{1,0:T(8,128)}, u32[]{:S(2)}) copy-start(f32[512,768]{1,0:T(8,128)} %copy-done) | copy-start | bytes 4718596
  1013.5 45.1 %copy-start.51 = (bf16[12,64,128]{2,1,0:T(8,128)(2,1)S(1)}, bf16[12,64,128]{2,1,0:T(8,128)(2,1)}, u32[]{:S(2)}) copy-start(bf16[12,64,128]{2,1,0:T(8,128)(2,1)} %copy-done.50) | copy-start | bytes 589828
  1013.5 45.1 %copy-start.53 = (bf16[12,64,128]{2,1,0:T(8,128)(2,1)S(1)}, bf16[12,64,128]{2,1,0:T(8,128)(2,1)}, u32[]{:S(2)}) copy-start(bf16[12,64,128]{2,1,0:T(8,128)(2,1)} %copy-done.52) | copy-start | bytes 589828
  1013.5 45.1 %copy-start.69 = (bf16[12,64,128]{2,1,0:T(8,128)(2,1)S(1)}, bf16[12,64,128]{2,1,0:T(8,128)(2,1)}, u32[]{:S(2)}) copy-start(bf16[12,64,128]{2,1,0:T(8,128)(2,1)} %get-tuple-element.269) | copy-start | bytes 589828
  (243 other events, 1753.9 us)
Sparse Core Ops, SparseCore 0:
  10.5 36.8 all-gather.32
  49.3 24.0 all-gather.34
  75.9 58.8 all-gather.36
  137.0 38.9 all-gather.38
  177.7 33.9 all-gather.40
  213.5 24.0 all-gather.42
  240.0 58.8 all-gather.44
  301.3 38.9 all-gather.46
  556.1 48.0 reduce-scatter.24
  607.5 48.0 reduce-scatter.26
  659.5 36.7 reduce-scatter.12
  700.3 36.7 reduce-scatter.14
  740.5 53.8 reduce-scatter.20
  798.7 53.8 reduce-scatter.22
  855.9 76.4 reduce-scatter.16
  935.8 76.4 reduce-scatter.18
  1016.3 184.4 all-reduce.37
where the time goes:
time: 1220 us
  waiting for transfers between devices  659 us (54%)
  matrix products  319 us (26%)
  other arithmetic  92.2 us (8%)
  blocking collectives  63.8 us (5%)
  local copies, waits for them, and re-layouts  61.6 us (5%)
  between operations  20.1 us (2%)
    reduce_scatter x2, waiting for transfers between devices, reduce_grads(): lax.psum_scatter(gateup_grad.astype(jnp.bfloat16), 'zero', scatter_dimens...  160 us
    psum x1, waiting for transfers between devices, reduce_grads(): lax.psum(qkv_owned.astype(jnp.bfloat16), 'dp').astype(jnp.float32)  134 us
    reduce_scatter x2, waiting for transfers between devices, reduce_grads(): lax.psum_scatter(wdown_grad.astype(jnp.bfloat16), 'zero', scatter_dimensi...  116 us
    all_gather x2, waiting for transfers between devices, fetch_forward(): lax.all_gather(w_gate_up, 'zero', axis=0, tiled=True)  95.5 us
    dot_general x16, matrix products, rows_product(): lax.dot_general(left, right, (((0,), (0,)), ((), ())), preferred_element_...  84.3 us
    reduce_scatter x2, waiting for transfers between devices, reduce_grads(): lax.psum_scatter(wout_grad.astype(jnp.bfloat16), 'zero', scatter_dimensio...  79.3 us
    dot_general x16, matrix products, times_transpose(): lax.dot_general(left, right, (((1,), (1,)), ((), ())), preferred_element_...  78.1 us
    unnamed x2, blocking collectives  51.1 us
  transfers between devices with their start and end apart: 17, of which 14 were waited for; matrix products, arithmetic and copies ran while one was open for 19% of the time, Pallas kernels for 0%

commit v1 on v0

--- a/solution.py
+++ b/solution.py
@@ -1,8 +1,11 @@
+import functools
 import math
 
 import jax
 import jax.numpy as jnp
 from jax import lax
+from jax.experimental import pallas as pl
+from jax.experimental.pallas import tpu as pltpu
 from jax.sharding import PartitionSpec as P
 
 HEADS = 12
@@ -446,6 +449,538 @@
     return (short_acts[-1], long_acts[-1], short_grad, long_grad) + tuple(stacked)
 
 
+MESH = pl.DeviceIdType.MESH
+NT = (((1,), (1,)), ((), ()))
+NN = (((1,), (0,)), ((), ()))
+TN = (((0,), (0,)), ((), ()))
+VMEM_LIMIT = 64 * 2**20
+
+KINDS = {"qkv": (3, 96, 768), "out": (1, 96, 768), "gu": (6, 96, 1024), "dn": (3, 384, 256)}
+ARRIVE = [("qkv", 0), ("qkv", 1), ("qkv", 2), ("out", 0), ("gu", 0), ("gu", 3), ("gu", 1)]
+ARRIVE += [("gu", 4), ("gu", 2), ("gu", 5), ("dn", 0), ("dn", 1), ("dn", 2)]
+LINK_BYTES_PER_US = 43000.0
+
+
+def mm(left, right, dims):
+    return lax.dot_general(left, right, dims, preferred_element_type=jnp.float32)
+
+
+def flip(index, bit):
+    return index + bit - 2 * bit * lax.rem(lax.div(index, bit), 2)
+
+
+def row_loop(total, step, body):
+    def run(number, carry):
+        body(pl.multiple_of(number * step, step))
+        return carry
+
+    lax.fori_loop(0, total // step, run, 0)
+
+
+def fill_distance(ref, valid_count):
+    size = ref.shape[0]
+    i = lax.broadcasted_iota(jnp.int32, (size, size), 0)
+    j = lax.broadcasted_iota(jnp.int32, (size, size), 1)
+    ref[...] = jnp.where(j < valid_count, jnp.abs(i - j).astype(jnp.float32), 1e18)
+
+
+def attend_pair(qkv, mixed, lse, dist, slopes, pair, base, size):
+    lane = lax.broadcasted_iota(jnp.int32, (1, 128), 1)
+    lanes = lax.broadcasted_iota(jnp.int32, (size, 128), 1)
+    rows = pl.ds(base, size)
+    cols = pl.ds(pl.multiple_of(pair * 128, 128), 128)
+    q2, k2, v2 = qkv[0, rows, cols], qkv[1, rows, cols], qkv[2, rows, cols]
+    stats = lse[rows, :]
+    parts = []
+    for half in range(2):
+        head = 2 * pair + half
+        q_head = jnp.where((lane < 64) == (half == 0), q2, jnp.zeros_like(q2)) * jnp.bfloat16(0.125)
+        scores = mm(q_head, k2, NT) - slopes[head] * dist[...]
+        top = jnp.max(scores, axis=1, keepdims=True)
+        powers = jnp.exp(scores - top)
+        total = jnp.sum(powers, axis=1, keepdims=True)
+        parts.append(mm((powers * (1.0 / total)).astype(jnp.bfloat16), v2, NN))
+        stats = jnp.where(lanes == head, top + jnp.log(total), stats)
+    mixed[rows, cols] = jnp.where(lane < 64, parts[0], parts[1]).astype(jnp.bfloat16)
+    lse[rows, :] = stats
+
+
+def gelu_parts(t):
+    size = jnp.abs(t)
+    k = 1.0 / (1.0 + (0.3275911 * math.sqrt(0.5)) * size)
+    poly = ((((0.5307027145 * k - 0.7265760135) * k + 0.7107068705) * k - 0.142248368) * k + 0.127414796) * k
+    bell = jnp.exp(-0.5 * t * t)
+    tail = poly * bell
+    phi = jnp.where(t >= 0.0, 1.0 - tail, tail)
+    return phi, bell * (1.0 / math.sqrt(2.0 * math.pi))
+
+
+def norm_rows(summed, gain, bias):
+    center = summed - jnp.mean(summed, axis=1, keepdims=True)
+    spread = jnp.mean(center * center, axis=1, keepdims=True)
+    inverse = lax.rsqrt(spread + epsilon)
+    normed = center * inverse
+    return normed * gain + bias, normed, inverse
+
+
+class Weave:
+    def __init__(self):
+        self.events = []
+        self.done = 0
+        self.clock = 0.0
+
+    def add(self, ready, name, act):
+        self.events.append((ready, len(self.events), name, act))
+
+    def seal(self):
+        self.events.sort(key=lambda event: (event[0], event[1]))
+
+    def step(self, cost):
+        self.clock += cost
+        while self.done < len(self.events) and self.events[self.done][0] <= self.clock:
+            self.one()
+
+    def one(self):
+        event = self.events[self.done]
+        self.done += 1
+        self.clock = max(self.clock, event[0])
+        event[3]()
+
+    def need(self, name):
+        while any(event[2] == name for event in self.events[self.done :]):
+            self.one()
+
+    def rest(self):
+        while self.done < len(self.events):
+            self.one()
+
+
+def forward_kernel(
+    short_len, long_len, slopes,
+    w_qkv, w_out, w_gu, w_dn, vecs, x_short, x_long,
+    short_out, long_out, o_qkv, o_out, o_gu, o_dn, o_vec, o_x, o_act, o_mixed, o_lse, o_vhat, o_r1, o_hid,
+    o_da, o_db, o_inner, o_uhat, o_r2,
+    b_qkv, b_out, b_gu, b_dn, b_vec, vec, x, act, mixed, lse, hid, inner, da, db, summed, normed, r_st,
+    dist_l, dist_s,
+    loc_sem, x_send, x_recv, y_send, y_recv, z_send, z_recv, c_send, c_recv, w_sem, in_sem, save_sem,
+):
+    source = {"qkv": w_qkv, "out": w_out, "gu": w_gu, "dn": w_dn}
+    buffer = {"qkv": b_qkv, "out": b_out, "gu": b_gu, "dn": b_dn}
+    kept = {"qkv": o_qkv, "out": o_out, "gu": o_gu, "dn": o_dn}
+    long_rows, short_rows = dist_l.shape[0], dist_s.shape[0]
+    rows, width = x.shape
+    chunks = [("vec", 0, 0)] + [(kind, l, b) for l in range(LAYERS) for kind, b in ARRIVE]
+
+    me, z = lax.axis_index("zero"), lax.axis_index("dp")
+    core, across_x, across_y, across_z = flip(me, 1), flip(me, 2), flip(me, 4), flip(z, 1)
+    odd = lax.rem(z, 2)
+    far = flip(across_x, 4)
+    y_out = me + odd * (across_x - me)
+    y_in = across_y + odd * (far - across_y)
+    z_in = far + odd * (across_y - far)
+    partners = ((z, core), (z, across_x), (z, across_y), (across_z, me))
+
+    in_copies = [
+        pltpu.make_async_copy(x_long.at[0], x.at[pl.ds(0, long_rows)], in_sem.at[0]),
+        pltpu.make_async_copy(x_short.at[0], x.at[pl.ds(long_rows, short_rows)], in_sem.at[1]),
+    ]
+    for copy in in_copies:
+        copy.start()
+
+    barrier = pltpu.get_barrier_semaphore()
+    for partner in partners:
+        pl.semaphore_signal(barrier, inc=1, device_id=partner, device_id_type=MESH)
+    pl.semaphore_wait(barrier, 4)
+
+    def piece(k, owner):
+        kind, l, b = chunks[k]
+        if kind == "vec":
+            return b_vec.at[owner]
+        count = KINDS[kind][1]
+        return buffer[kind].at[l, b, pl.ds(pl.multiple_of(owner * count, count), count)]
+
+    def own(k):
+        kind, l, b = chunks[k]
+        if kind == "vec":
+            return vecs
+        columns = KINDS[kind][2]
+        return source[kind].at[l, :, pl.ds(b * columns, columns)]
+
+    def send(k, src, owner, send_sem, recv_sem, partner):
+        return pltpu.make_async_remote_copy(
+            src_ref=src, dst_ref=piece(k, owner), send_sem=send_sem, recv_sem=recv_sem,
+            device_id=partner, device_id_type=MESH,
+        )
+
+    def loc(k):
+        return pltpu.make_async_copy(own(k), piece(k, me), loc_sem.at[k])
+
+    def x_copy(k):
+        return send(k, own(k), me, x_send.at[k], x_recv.at[k], partners[1])
+
+    def y_copy(k):
+        return send(k, piece(k, y_out), y_out, y_send.at[k], y_recv.at[k], partners[2])
+
+    def z_copy(k):
+        return send(k, piece(k, y_in), y_in, z_send.at[k], z_recv.at[k], partners[3])
+
+    def c_copy(k, j):
+        owner = (me, across_x, y_in, z_in)[j]
+        src = own(k) if j == 0 else piece(k, owner)
+        return send(k, src, owner, c_send.at[k, j], c_recv.at[k, j], partners[0])
+
+    def after_x(k):
+        loc(k).wait()
+        x_copy(k).wait_recv()
+        y_copy(k).start()
+        c_copy(k, 1).start()
+
+    def after_y(k):
+        y_copy(k).wait_recv()
+        z_copy(k).start()
+        c_copy(k, 2).start()
+
+    def after_z(k):
+        z_copy(k).wait_recv()
+        c_copy(k, 3).start()
+
+    def keep(k):
+        kind, l, b = chunks[k]
+        return pltpu.make_async_copy(buffer[kind].at[l, b], kept[kind].at[l, b], w_sem.at[k])
+
+    def whole(k):
+        for j in range(4):
+            c_copy(k, j).wait_recv()
+        if chunks[k][0] != "vec":
+            keep(k).start()
+
+    weave = Weave()
+    arrival = 2.0
+    for k, (kind, l, b) in enumerate(chunks):
+        loc(k).start()
+        x_copy(k).start()
+        c_copy(k, 0).start()
+        held = 16 * 128 if kind == "vec" else KINDS[kind][1] * KINDS[kind][2]
+        span = 2 * held / LINK_BYTES_PER_US
+        arrival += span
+        weave.add(arrival, "", functools.partial(after_x, k))
+        weave.add(arrival + span + 2.0, "", functools.partial(after_y, k))
+        weave.add(arrival + 2 * span + 4.0, "", functools.partial(after_z, k))
+        weave.add(arrival + 2 * span + 6.0, (kind, l, b), functools.partial(whole, k))
+    weave.seal()
+
+    saves = []
+
+    def save(src, dst):
+        copy = pltpu.make_async_copy(src, dst, save_sem.at[len(saves)])
+        copy.start()
+        saves.append([copy, False])
+        return len(saves) - 1
+
+    def saved(number):
+        if not saves[number][1]:
+            saves[number][0].wait()
+            saves[number][1] = True
+
+    fill_distance(dist_l, long_len[0])
+    fill_distance(dist_s, short_len[0])
+    lse[...] = jnp.zeros_like(lse)
+    position = lax.broadcasted_iota(jnp.int32, (rows, 1), 0)
+    bound = jnp.where(position < long_rows, long_len[0], short_len[0] + long_rows)
+    valid = (position < bound).astype(jnp.float32)
+
+    weave.need(("vec", 0, 0))
+    spread = []
+    owners = b_vec.shape[0]
+    each = width // owners
+    total = jnp.zeros(vec.shape, jnp.float32)
+    for owner in range(owners):
+        i = lax.broadcasted_iota(jnp.int32, (128, width), 0)
+        j = lax.broadcasted_iota(jnp.int32, (128, width), 1)
+        place = ((j == i + owner * each) & (i < each)).astype(jnp.bfloat16)
+        total = total + mm(b_vec[owner], place, NN)
+    vec[...] = total
+    save(vec, o_vec)
+    for copy in in_copies:
+        copy.wait()
+
+    def vector(l, number):
+        return vec[pl.ds(l * 8 + number, 1), :]
+
+    held_saves = {}
+    for l in range(LAYERS):
+        for part in range(3):
+            weave.need(("qkv", l, part))
+            if part == 0 and "act" in held_saves:
+                for number in held_saves["act"]:
+                    saved(number)
+            projected = mm(x[...], b_qkv[l, part], NN)
+            if part == 0:
+                projected = projected + vector(l, 0)
+            if part == 2:
+                projected = projected + vector(l, 1)
+            act[part] = projected.astype(jnp.bfloat16)
+            weave.step(1.5)
+        now = [save(act, o_act.at[l])]
+
+        if "mixed" in held_saves:
+            for number in held_saves["mixed"]:
+                saved(number)
+        for group in range(3):
+            def one_pair(pair, carry):
+                attend_pair(act, mixed, lse, dist_l, slopes, pair, 0, long_rows)
+                attend_pair(act, mixed, lse, dist_s, slopes, pair, long_rows, short_rows)
+                return carry
+
+            lax.fori_loop(2 * group, 2 * group + 2, one_pair, 0)
+            weave.step(4.0)
+        held_saves["act"] = now
+        held_saves["mixed"] = [save(mixed, o_mixed.at[l]), save(lse, o_lse.at[l])]
+
+        weave.need(("out", l, 0))
+        summed[...] = mm(mixed[...], b_out[l, 0], NN)
+        if "normed" in held_saves:
+            for number in held_saves["normed"]:
+                saved(number)
+
+        def first_norm(r0):
+            part = pl.ds(r0, 128)
+            out, unit, inverse = norm_rows(
+                summed[part, :] + vector(l, 2) + x[part, :].astype(jnp.float32), vector(l, 3), vector(l, 4)
+            )
+            hid[part, :] = out.astype(jnp.bfloat16)
+            normed[part, :] = unit
+            r_st[part, :] = jnp.broadcast_to(inverse, (128, 128))
+
+        if "hid" in held_saves:
+            for number in held_saves["hid"]:
+                saved(number)
+        row_loop(rows, 128, first_norm)
+        held_saves["normed"] = [save(normed, o_vhat.at[l]), save(r_st, o_r1.at[l])]
+        held_saves["hid"] = [save(hid, o_hid.at[l])]
+        weave.step(2.5)
+
+        if "inner" in held_saves:
+            for number in held_saves["inner"]:
+                saved(number)
+        half = b_gu.shape[1] // 2
+        span = b_gu.shape[3]
+        now = []
+        for b in range(half):
+            weave.need(("gu", l, b))
+            weave.need(("gu", l, half + b))
+            if "gelu" in held_saves:
+                for number in held_saves["gelu"]:
+                    saved(number)
+
+            def gelu_block(j, carry):
+                c0 = pl.multiple_of(j * 256, 256)
+                cols = pl.ds(c0, 256)
+                gate = mm(hid[...], b_gu[l, b, :, cols], NN)
+                up = mm(hid[...], b_gu[l, half + b, :, cols], NN)
+                phi, density = gelu_parts(gate)
+                value = gate * phi
+                inner[b, :, cols] = (value * up).astype(jnp.bfloat16)
+                db[:, cols] = value.astype(jnp.bfloat16)
+                da[:, cols] = (up * (phi + gate * density)).astype(jnp.bfloat16)
+                return carry
+
+            lax.fori_loop(0, span // 256, gelu_block, 0)
+            held_saves["gelu"] = [save(da, o_da.at[l, b]), save(db, o_db.at[l, b])]
+            now.append(save(inner.at[b], o_inner.at[l, b]))
+            weave.step(6.0)
+        held_saves["inner"] = now
+
+        blocks = b_dn.shape[1]
+        wide = b_dn.shape[3]
+        for b in range(blocks):
+            weave.need(("dn", l, b))
+            product = mm(inner[0], b_dn[l, b, pl.ds(0, span), :], NN)
+            for part in range(1, half):
+                product = product + mm(inner[part], b_dn[l, b, pl.ds(part * span, span), :], NN)
+            summed[:, pl.ds(b * wide, wide)] = product
+            weave.step(1.5)
+
+        for number in held_saves["normed"]:
+            saved(number)
+        if "x" in held_saves:
+            for number in held_saves["x"]:
+                saved(number)
+
+        def second_norm(r0):
+            part = pl.ds(r0, 128)
+            out, unit, inverse = norm_rows(
+                summed[part, :] + vector(l, 5) + hid[part, :].astype(jnp.float32), vector(l, 6), vector(l, 7)
+            )
+            place = lax.broadcasted_iota(jnp.int32, (128, 1), 0) + r0
+            limit = jnp.where(place < long_rows, long_len[0], short_len[0] + long_rows)
+            x[part, :] = jnp.where(place < limit, out, 0.0).astype(jnp.bfloat16)
+            normed[part, :] = unit
+            r_st[part, :] = jnp.broadcast_to(inverse, (128, 128))
+
+        row_loop(rows, 128, second_norm)
+        held_saves["normed"] = [save(normed, o_uhat.at[l]), save(r_st, o_r2.at[l])]
+        if l < LAYERS - 1:
+            held_saves["x"] = [save(x, o_x)]
+        weave.step(2.5)
+
+    save(x.at[pl.ds(0, long_rows)], long_out.at[0])
+    save(x.at[pl.ds(long_rows, short_rows)], short_out.at[0])
+    weave.rest()
+    for number in range(len(saves)):
+        saved(number)
+    for k in range(len(chunks)):
+        x_copy(k).wait_send()
+        y_copy(k).wait_send()
+        z_copy(k).wait_send()
+        for j in range(4):
+            c_copy(k, j).wait_send()
+        if chunks[k][0] != "vec":
+            keep(k).wait()
+
+
+def forward(short_len, long_len, params, short_in, long_in):
+    (w_qkv, q_bias, v_bias, w_out, out_bias, gain_one, bias_one, w_gu, w_dn, down_bias, gain_two, bias_two) = params
+    shard, width = w_qkv.shape[1], w_qkv.shape[2] // 3
+    owners = width // shard
+    hidden = w_dn.shape[1] * owners
+    packed = jnp.stack([q_bias, v_bias, out_bias, gain_one, bias_one, down_bias, gain_two, bias_two], axis=1)
+    packed = jnp.pad(packed.reshape(16, shard), ((0, 0), (0, 128 - shard)))
+    rows = short_in.shape[1] + long_in.shape[1]
+    low, full = jnp.bfloat16, jnp.float32
+    sizes = {k: (LAYERS, n, owners * r, c) for k, (n, r, c) in KINDS.items()}
+    half, span = sizes["gu"][1] // 2, sizes["gu"][3]
+    count = 1 + LAYERS * len(ARRIVE)
+    out_shape = [
+        jax.ShapeDtypeStruct(short_in.shape, low),
+        jax.ShapeDtypeStruct(long_in.shape, low),
+        jax.ShapeDtypeStruct(sizes["qkv"], low),
+        jax.ShapeDtypeStruct(sizes["out"], low),
+        jax.ShapeDtypeStruct(sizes["gu"], low),
+        jax.ShapeDtypeStruct(sizes["dn"], low),
+        jax.ShapeDtypeStruct((16, width), full),
+        jax.ShapeDtypeStruct((rows, width), low),
+        jax.ShapeDtypeStruct((LAYERS, 3, rows, width), low),
+        jax.ShapeDtypeStruct((LAYERS, rows, width), low),
+        jax.ShapeDtypeStruct((LAYERS, rows, 128), full),
+        jax.ShapeDtypeStruct((LAYERS, rows, width), full),
+        jax.ShapeDtypeStruct((LAYERS, rows, 128), full),
+        jax.ShapeDtypeStruct((LAYERS, rows, width), low),
+        jax.ShapeDtypeStruct((LAYERS, half, rows, span), low),
+        jax.ShapeDtypeStruct((LAYERS, half, rows, span), low),
+        jax.ShapeDtypeStruct((LAYERS, half, rows, span), low),
+        jax.ShapeDtypeStruct((LAYERS, rows, width), full),
+        jax.ShapeDtypeStruct((LAYERS, rows, 128), full),
+    ]
+    dma = pltpu.SemaphoreType.DMA
+    scratch = [pltpu.VMEM(sizes[k], low) for k in ("qkv", "out", "gu", "dn")]
+    scratch += [
+        pltpu.VMEM((owners, 16, 128), low),
+        pltpu.VMEM((16, width), full),
+        pltpu.VMEM((rows, width), low),
+        pltpu.VMEM((3, rows, width), low),
+        pltpu.VMEM((rows, width), low),
+        pltpu.VMEM((rows, 128), full),
+        pltpu.VMEM((rows, width), low),
+        pltpu.VMEM((half, rows, span), low),
+        pltpu.VMEM((rows, span), low),
+        pltpu.VMEM((rows, span), low),
+        pltpu.VMEM((rows, width), full),
+        pltpu.VMEM((rows, width), full),
+        pltpu.VMEM((rows, 128), full),
+        pltpu.VMEM((long_in.shape[1],) * 2, full),
+        pltpu.VMEM((short_in.shape[1],) * 2, full),
+    ]
+    scratch += [dma((count,))] * 7 + [dma((count, 4))] * 2 + [dma((count,)), dma((2,)), dma((48,))]
+    smem = pl.BlockSpec(memory_space=pltpu.SMEM)
+    hbm = pl.BlockSpec(memory_space=pl.ANY)
+    return pl.pallas_call(
+        forward_kernel,
+        out_shape=out_shape,
+        in_specs=[smem] * 3 + [hbm] * 7,
+        out_specs=[hbm] * len(out_shape),
+        scratch_shapes=scratch,
+        compiler_params=pltpu.CompilerParams(
+            collective_id=0, has_side_effects=True, vmem_limit_bytes=VMEM_LIMIT
+        ),
+        cost_estimate=pl.CostEstimate(flops=26 * 10**9, bytes_accessed=2 * 10**8, transcendentals=10**7),
+    )(short_len, long_len, head_slopes(HEADS), w_qkv, w_out, w_gu, w_dn, packed, short_in, long_in)
+
+
+def backward_layer(l, state, lengths, valid, grad_rows_in, rows_of):
+    s = {name: value[l][rows_of] if name != "act" and name not in ("da", "db", "inner") else value[l][:, rows_of] for name, value in state["rows"].items()}
+    wq, wo, wg, wd = (state["w"][n][l] for n in ("qkv", "out", "gu", "dn"))
+    cat = lambda w: jnp.concatenate([w[i] for i in range(w.shape[0])], axis=1)
+    w_qkv, w_out, w_gu, w_dn = cat(wq), cat(wo), cat(wg), cat(wd)
+    vec = state["vec"][l * 8 : l * 8 + 8]
+    gain_one, gain_two = vec[3], vec[6]
+    row_count = grad_rows_in.shape[0]
+    cat2 = lambda a: jnp.concatenate([a[i] for i in range(a.shape[0])], axis=1)
+    da, db, inner = cat2(s["da"]), cat2(s["db"]), cat2(s["inner"])
+    score_scale = 0.125
+    gn = grad_rows_in * valid
+    grad_u, gaintwo, biastwo = normalize_back(gn, s["uhat"], s["r2"][:, :1], gain_two)
+    gd = grad_u.astype(jnp.bfloat16)
+    bdown = jnp.sum(gd, axis=0, dtype=jnp.float32)
+    wdown = rows_product(inner, gd)
+    gi = times_transpose(gd, w_dn)
+    ggu = jnp.concatenate([gi * da.astype(jnp.float32), gi * db.astype(jnp.float32)], axis=1).astype(jnp.bfloat16)
+    wgu = rows_product(s["hid"], ggu)
+    gh = grad_u + times_transpose(ggu, w_gu)
+    gv, gainone, biasone = normalize_back(gh, s["vhat"], s["r1"][:, :1], gain_one)
+    gb = gv.astype(jnp.bfloat16)
+    bout = jnp.sum(gb, axis=0, dtype=jnp.float32)
+    wout = rows_product(s["mixed"], gb)
+    gm = times_transpose(gb, w_out).astype(jnp.bfloat16)
+    n = row_count
+    q, k, v = (split_heads(s["act"][i], 1, n) for i in range(3))
+    gmh = split_heads(gm, 1, n)
+    pos = jnp.arange(n)
+    dist = jnp.abs(pos[:, None] - pos[None, :]).astype(jnp.float32)
+    sc = jnp.einsum("sqhd,skhd->shqk", q, k, preferred_element_type=jnp.float32) * score_scale
+    sc = sc - head_slopes(HEADS)[None, :, None, None] * dist[None, None]
+    sc = jnp.where((pos[None, :] < lengths[:, None])[:, None, None, :], sc, masked_score)
+    probs = jnp.exp(sc - s["lse"][:, :HEADS].T[None, :, :, None])
+    pl_ = probs.astype(jnp.bfloat16)
+    gp = jnp.einsum("sqhd,skhd->shqk", gmh, v, preferred_element_type=jnp.float32)
+    gs = (probs * (gp - jnp.sum(probs * gp, axis=-1, keepdims=True))).astype(jnp.bfloat16)
+    gq = (jnp.einsum("shqk,skhd->sqhd", gs, k, preferred_element_type=jnp.float32) * score_scale).astype(jnp.bfloat16).reshape(n, -1)
+    gk = (jnp.einsum("shqk,sqhd->skhd", gs, q, preferred_element_type=jnp.float32) * score_scale).astype(jnp.bfloat16).reshape(n, -1)
+    gvv = jnp.einsum("shqk,sqhd->skhd", pl_, gmh, preferred_element_type=jnp.float32).astype(jnp.bfloat16).reshape(n, -1)
+    gp3 = jnp.concatenate([gq, gk, gvv], axis=1)
+    wqkv = rows_product(s["x"], gp3)
+    gx = gv + times_transpose(gp3, w_qkv)
+    terms = (wqkv, jnp.sum(gq, axis=0, dtype=jnp.float32), jnp.sum(gvv, axis=0, dtype=jnp.float32), wout, bout, gainone, biasone, wgu, wdown, bdown, gaintwo, biastwo)
+    return gx, terms
+
+
+def per_device_fused(
+    short_in, long_in, short_lengths, long_lengths, w_qkv, q_bias, v_bias, w_out, out_bias, norm1_gain, norm1_bias,
+    w_gate_up, w_down, down_bias, norm2_gain, norm2_bias, short_cot, long_cot,
+):
+    params = (w_qkv, q_bias, v_bias, w_out, out_bias, norm1_gain, norm1_bias, w_gate_up, w_down, down_bias, norm2_gain, norm2_bias)
+    (short_out, long_out, k_qkv, k_out, k_gu, k_dn, vec, x1, act, mixed, lse, vhat, r1, hid, da, db, inner, uhat, r2) = forward(short_lengths, long_lengths, params, short_in, long_in)
+    x = jnp.stack([jnp.concatenate([long_in[0], short_in[0]]), x1])
+    state = {
+        "rows": dict(x=x, act=act, mixed=mixed, lse=lse, vhat=vhat, r1=r1, hid=hid, da=da, db=db, inner=inner, uhat=uhat, r2=r2),
+        "w": dict(qkv=k_qkv, out=k_out, gu=k_gu, dn=k_dn),
+        "vec": vec,
+    }
+    nl, ns = long_in.shape[1], short_in.shape[1]
+    grads = [long_cot[0].astype(jnp.float32), short_cot[0].astype(jnp.float32)]
+    spans = [slice(0, nl), slice(nl, nl + ns)]
+    lens = [long_lengths, short_lengths]
+    valids = [(jnp.arange(n) < le[0]).astype(jnp.float32)[:, None] for n, le in ((nl, long_lengths), (ns, short_lengths))]
+    reduced = [None] * LAYERS
+    for l in reversed(range(LAYERS)):
+        terms = [None, None]
+        for b in range(2):
+            grads[b], terms[b] = backward_layer(l, state, lens[b], valids[b], grads[b], spans[b])
+        reduced[l] = reduce_grads(jax.tree.map(jnp.add, *terms))
+    stacked = [jnp.stack([reduced[l][m] for l in range(LAYERS)]) for m in range(len(params))]
+    return (short_out, long_out, grads[1][None], grads[0][None]) + tuple(stacked)
+
+
 def solution(mesh):
     placed = (
         P(("dp", "zero"), None, None),
@@ -467,8 +1002,9 @@
         P(("dp", "zero"), None, None),
         P(("dp", "zero"), None, None),
     )
+    fused = mesh.shape["zero"] == 8 and mesh.shape["dp"] == 4
     return jax.shard_map(
-        per_device,
+        per_device_fused if fused else per_device,
         mesh=mesh,
         in_specs=placed,
         out_specs=(

time: 1220 us -> 1050 us (0.86)
  waiting for transfers between devices: 659 us -> 411 us
  Pallas kernels: 0 us -> 155 us
  matrix products: 319 us -> 216 us
  local copies, waits for them, and re-layouts: 61.6 us -> 135 us
  blocking collectives: 63.8 us -> 39.7 us
  other arithmetic: 92.2 us -> 72.5 us
    all_gather x8 -> x0, waiting for transfers between devices: 155 us -> none  [the longest x2 95.5 us: fetch_forward(): lax.all_gather(w_gate_up, 'zero', axis=0, tiled=True)]
    pallas_call x0 -> x1, Pallas kernels: none -> 155 us  [forward(): pl.pallas_call(forward_kernel, out_shape=out_shape, in_specs=[smem] * 3 +...]
    dot_general x36 -> x20, matrix products: 133 us -> 51.4 us  [the longest x4 17.7 us: backward_layer(): jnp.einsum('sqhd,skhd->shqk', q, k, preferred_element_type=jnp.float32)]
    reduce_scatter x2, waiting for transfers between devices: 79.3 us -> 32.9 us  [reduce_grads(): lax.psum_scatter(wout_grad.astype(jnp.bfloat16), 'zero', scatter_dimensio...]
    convert_element_type x32 -> x8, other arithmetic: 62.6 us -> 16.9 us  [the longest x4 14 us: backward_layer(): (probs * (gp - jnp.sum(probs * gp, axis=-1, keepdims=True))).astype(jnp.b...]
    squeeze x0 -> x15, local copies, waits for them, and re-layouts: none -> 38.9 us  [the longest x10 16.8 us: backward_layer(): cat2 = lambda a: jnp.concatenate([a[i] for i in range(a.shape[0])], axis=1)]
    psum x1, waiting for transfers between devices: 134 us -> 103 us  [reduce_grads(): lax.psum(qkv_owned.astype(jnp.bfloat16), 'dp').astype(jnp.float32)]
    unnamed x2 -> x1, blocking collectives: 51.1 us -> 25.9 us
  transfers between devices with their start and end apart: 17 -> 9, of which waited for: 14 -> 6; matrix products, arithmetic and copies ran while one was open for 19% -> 23% of each run, Pallas kernels for 0% -> 0%
where the time goes in v1:
time: 1050 us
  waiting for transfers between devices  411 us (39%)
  matrix products  216 us (21%)
  Pallas kernels  155 us (15%)
  local copies, waits for them, and re-layouts  135 us (13%)
  other arithmetic  72.5 us (7%)
  blocking collectives  39.7 us (4%)
  between operations  17.9 us (2%)
    reduce_scatter x2, waiting for transfers between devices, reduce_grads(): lax.psum_scatter(gateup_grad.astype(jnp.bfloat16), 'zero', scatter_dimens...  160 us
    pallas_call x1, Pallas kernels, forward(): pl.pallas_call(forward_kernel, out_shape=out_shape, in_specs=[smem] * 3 +...  155 us
    reduce_scatter x2, waiting for transfers between devices, reduce_grads(): lax.psum_scatter(wdown_grad.astype(jnp.bfloat16), 'zero', scatter_dimensi...  115 us
    psum x1, waiting for transfers between devices, reduce_grads(): lax.psum(qkv_owned.astype(jnp.bfloat16), 'dp').astype(jnp.float32)  103 us
    dot_general x16, matrix products, rows_product(): lax.dot_general(left, right, (((0,), (0,)), ((), ())), preferred_element_...  83.4 us
    dot_general x16, matrix products, times_transpose(): lax.dot_general(left, right, (((1,), (1,)), ((), ())), preferred_element_...  81.2 us
    unnamed x361, local copies, waits for them, and re-layouts  43.7 us
    reduce_scatter x2, waiting for transfers between devices, reduce_grads(): lax.psum_scatter(wout_grad.astype(jnp.bfloat16), 'zero', scatter_dimensio...  32.9 us
  transfers between devices with their start and end apart: 9, of which 6 were waited for; matrix products, arithmetic and copies ran while one was open for 23% of the time, Pallas kernels for 0%

profile of v1, /device:TPU:0, one launch (start us, length us, event | category | flops | bytes accessed | tf_op | source)
XLA Modules:
  0.0 1048.1 jit_solution(6967325632383786778)
XLA Ops:
  16.2 154.8 %shard_map.342 = (bf16[1,128,768]{2,1,0:T(8,128)(2,1)}, bf16[1,512,768]{2,1,0:T(8,128)(2,1)}, bf16[2,3,768,768]{3,2,1,0:T(8,128)(2,1)}, bf16[2,1,768,768]{3,2,1,...) custom-call(s32[1]{0:T(128)} %copy.203.short_len, ...), custom_call_target="tpu_custom_call" | custom-call | flops 25999998976 | bytes 200000000 | tf_op jit(solution)/shard_map/pallas_call | solution.py:897
  186.2 6.3 slice_bitcast_fusion.2
  203.7 6.1 slice_bitcast_fusion.10
  209.9 6.0 bitcast_dynamic-update-slice_fusion.5
  236.1 5.4 fusion.142
  263.4 8.5 multiply_convert_fusion.5
  271.9 12.3 %fusion.52 = (f32[768]{0:T(1024)}, f32[512]{0:T(512)S(1)}, f32[512]{0:T(512)S(1)}, f32[768]{0:T(1024)}, f32[512,768]{1,0:T(8,128)S(1)}) fusion(f32[2,640,768]{2,1,0:T(8,128)S(1)} %copy-done.7, f32[768]{0:T(1024)S(1)} %get-tuple-element.136, f32[512,768]{1,0:T(8,128)} %get-tuple-element.185, bf16[768,6144]{1,0:T(8,128)(2,1)} %get-tuple-element.195, ...), kind=kOutput, calls=%fused_computation.99 | convolution fusion | flops 4847563776 | bytes 20460544 | tf_op jit(solution)/shard_map/dot_general | solution.py:33
  292.3 8.1 multiply_reduce_fusion.1
  300.4 7.3 convert_reduce_fusion.4
  307.7 7.0 multiply_convert_fusion.1
  339.2 4.2 fusion.48
  351.5 8.3 fusion.134
  370.4 8.2 multiply_convert_fusion.3
  378.6 13.4 %fusion.44 = (f32[768]{0:T(1024)}, f32[512]{0:T(512)S(1)}, f32[512]{0:T(512)S(1)}, f32[768]{0:T(1024)}, f32[512,768]{1,0:T(8,128)}) fusion(f32[2,640,768]{2,1,0:T(8,128)S(1)} %copy-done.8, f32[768]{0:T(1024)S(1)} %get-tuple-element.134, f32[512,768]{1,0:T(8,128)} %get-tuple-element.181, bf16[768,6144]{1,0:T(8,128)(2,1)} %copy-done.102, ...), kind=kOutput, calls=%fused_computation.85 | convolution fusion | flops 4847563776 | bytes 20460544 | tf_op jit(solution)/shard_map/dot_general | solution.py:33
  400.8 6.4 fusion.212
  407.2 8.6 multiply_reduce_fusion
  415.8 6.8 multiply_convert_fusion
  431.8 4.0 copy.170
  446.5 4.4 slice_bitcast_fusion.1
  461.7 4.7 fusion.15
  470.3 14.8 %fusion.13 = f32[768,6144]{1,0:T(8,128)} fusion(bf16[512,3072]{1,0:T(8,128)(2,1)} %get-tuple-element.227, bf16[512,3072]{1,0:T(8,128)(2,1)} %copy-done.13, bf16[2,640,768]{2,1,0:T(8,128)(2,1)} %get-tuple-element.52), kind=kOutput, calls=%fused_computation.33 | convolution fusion | flops 4844421120 | bytes 25952256 | tf_op jit(solution)/shard_map/dot_general | solution.py:27
  485.1 10.8 %add_convert_fusion = bf16[768,6144]{1,0:T(8,128)(2,1)} fusion(f32[768,6144]{1,0:T(8,128)} %fusion.13, bf16[128,3072]{1,0:T(8,128)(2,1)S(1)} %copy-done.88, bf16[128,3072]{1,0:T(8,128)(2,1)S(1)} %copy-done.86, bf16[2,640,768]{2,1,0:T(8,128)(2,1)} %get-tuple-element.52), kind=kOutput, calls=%fused_computation | convolution fusion | flops 1220542464 | bytes 30081024 | tf_op jit(solution)/shard_map/dot_general | solution.py:27
  496.3 15.1 %fusion.11 = f32[768,6144]{1,0:T(8,128)} fusion(bf16[512,3072]{1,0:T(8,128)(2,1)} %copy-done.15, bf16[512,3072]{1,0:T(8,128)(2,1)} %copy-done.14, bf16[2,640,768]{2,1,0:T(8,128)(2,1)} %get-tuple-element.52), kind=kOutput, calls=%fused_computation.31 | convolution fusion | flops 4844421120 | bytes 25952256 | tf_op jit(solution)/shard_map/dot_general | solution.py:27
  511.3 11.1 %add_convert_fusion.1 = bf16[768,6144]{1,0:T(8,128)(2,1)} fusion(f32[768,6144]{1,0:T(8,128)} %fusion.11, bf16[128,3072]{1,0:T(8,128)(2,1)S(1)} %copy-done.94, bf16[128,3072]{1,0:T(8,128)(2,1)S(1)} %copy-done.92, bf16[2,640,768]{2,1,0:T(8,128)(2,1)} %get-tuple-element.52), kind=kOutput, calls=%fused_computation.1 | convolution fusion | flops 1220542464 | bytes 30081024 | tf_op jit(solution)/shard_map/dot_general | solution.py:27
  533.3 32.9 %reduce-scatter.13.cloned.1.call-done = bf16[96,768]{1,0:T(8,128)(2,1)} async-done(((bf16[768,768]{1,0:T(8,128)(2,1)}), bf16[96,768]{1,0:T(8,128)(2,1)}) %reduce-scatter.13.cloned.1.call-update) | async-done | bytes 147472 | tf_op jit(solution)/shard_map/reduce_scatter | solution.py:330
  566.2 57.8 %reduce-scatter.23.cloned.1.call-done = bf16[384,768]{1,0:T(8,128)(2,1)} async-done(((bf16[3072,768]{1,0:T(8,128)(2,1)}), bf16[384,768]{1,0:T(8,128)(2,1)}) %reduce-scatter.23.cloned.1.call-update) | async-done | bytes 589840 | tf_op jit(solution)/shard_map/reduce_scatter | solution.py:345
  624.0 57.6 %reduce-scatter.21.cloned.1.call-done = bf16[384,768]{1,0:T(8,128)(2,1)} async-done(((bf16[3072,768]{1,0:T(8,128)(2,1)}), bf16[384,768]{1,0:T(8,128)(2,1)}) %reduce-scatter.21.cloned.1.call-update) | async-done | bytes 589840 | tf_op jit(solution)/shard_map/reduce_scatter | solution.py:345
  681.6 80.0 %reduce-scatter.19.cloned.1.call-done = bf16[96,6144]{1,0:T(8,128)(2,1)} async-done(((bf16[768,6144]{1,0:T(8,128)(2,1)}), bf16[96,6144]{1,0:T(8,128)(2,1)}) %reduce-scatter.19.cloned.1.call-update) | async-done | bytes 1179664 | tf_op jit(solution)/shard_map/reduce_scatter | solution.py:342
  761.6 80.0 %reduce-scatter.17.cloned.1.call-done = bf16[96,6144]{1,0:T(8,128)(2,1)} async-done(((bf16[768,6144]{1,0:T(8,128)(2,1)}), bf16[96,6144]{1,0:T(8,128)(2,1)}) %reduce-scatter.17.cloned.1.call-update) | async-done | bytes 1179664 | tf_op jit(solution)/shard_map/reduce_scatter | solution.py:342
  854.6 25.9 %all-reduce.17 = (bf16[768]{0:T(1024)(128)(2,1)S(1)}, bf16[768]{0:T(1024)(128)(2,1)S(1)}, bf16[768]{0:T(1024)(128)(2,1)S(1)}, bf16[768]{0:T(1024)(128)(2,1)}, bf...) all-reduce(bf16[768]{0:T(1024)(128)(2,1)} %convert_element_type.549, ...), channel_id=5, replica_groups=mesh['dp'=4,'zero'=8] {'zero'}, use_global_device_ids=true, to_apply=%region_30.31.clone | all-reduce | flops 12288 | bytes 49152
  896.5 13.8 %all-reduce.18 = (bf16[1,96]{1,0:T(2,128)(2,1)}, bf16[1,96]{1,0:T(2,128)(2,1)}, bf16[1,96]{1,0:T(2,128)(2,1)}, bf16[1,96]{1,0:T(2,128)(2,1)}, bf16[1,96]{1,0:T(2...) all-reduce(bf16[1,96]{1,0:T(2,128)(2,1)S(1)} %dynamic-slice_bitcast, ...), channel_id=1, replica_groups=mesh['dp'=4,'zero'=8] {'dp'}, use_global_device_ids=true, to_apply=%region_31.32 | all-reduce | flops 1536 | bytes 6144 | tf_op jit(solution)/shard_map/psum | solution.py:374
  927.3 102.9 %all-reduce.22.cloned.1.call-done = (bf16[1,96,2304]{1,2,0:T(8,128)(2,1)}, bf16[1,96,2304]{1,2,0:T(8,128)(2,1)}, bf16[1,96,768]{2,1,0:T(8,128)(2,1)}, bf16[1,96,...) async-done(((bf16[1,96,2304]{1,2,0:T(8,128)(2,1)}, ...) | async-done | bytes 4718608 | tf_op jit(solution)/shard_map/psum | solution.py:373
  (550 shorter events, 236.7 us)
Async XLA Ops:
  7.2 521.8 %reduce-scatter.27.cloned.1.call-start = ((), (), s32[]{:S(2)}) async-start(), calls=%async_computation.15 | async-start | bytes 3981312
  196.1 26.2 %slice-start = ((s8[18874368]{0:T(1024)(128)(4,1)}), s8[2097152]{0:T(1024)(128)(4,1)S(1)}, s32[]{:S(2)}) async-start(s8[18874368]{0:T(1024)(128)(4,1)} %bitcast.518), calls=%async_computation.17 | async-start | bytes 4194304
  203.7 18.6 %slice-start.1 = ((s8[18874368]{0:T(1024)(128)(4,1)}), s8[4194304]{0:T(1024)(128)(4,1)S(1)}, s32[]{:S(2)}) async-start(s8[18874368]{0:T(1024)(128)(4,1)} %bitcast.518), calls=%async_computation.18 | async-start | bytes 8388608
  203.7 18.6 %slice-start.2 = ((s8[18874368]{0:T(1024)(128)(4,1)}), s8[4194304]{0:T(1024)(128)(4,1)S(1)}, s32[]{:S(2)}) async-start(s8[18874368]{0:T(1024)(128)(4,1)} %bitcast.518), calls=%async_computation.19 | async-start | bytes 8388608
  203.7 18.6 %slice-start.3 = ((s8[18874368]{0:T(1024)(128)(4,1)}), s8[4194304]{0:T(1024)(128)(4,1)S(1)}, s32[]{:S(2)}) async-start(s8[18874368]{0:T(1024)(128)(4,1)} %bitcast.518), calls=%async_computation.20 | async-start | bytes 8388608
  209.9 23.5 %copy-start.34 = (bf16[3072,256]{1,0:T(8,128)(2,1)}, bf16[3072,256]{1,0:T(8,128)(2,1)S(1)}, u32[]{:S(2)}) copy-start(bf16[3072,256]{1,0:T(8,128)(2,1)S(1)} %get-tuple-element.209) | copy-start | bytes 4718596
  209.9 23.5 %copy-start.36 = (bf16[3072,256]{1,0:T(8,128)(2,1)}, bf16[3072,256]{1,0:T(8,128)(2,1)S(1)}, u32[]{:S(2)}) copy-start(bf16[3072,256]{1,0:T(8,128)(2,1)S(1)} %get-tuple-element.210) | copy-start | bytes 4718596
  209.9 23.5 %copy-start.38 = (bf16[3072,256]{1,0:T(8,128)(2,1)}, bf16[3072,256]{1,0:T(8,128)(2,1)S(1)}, u32[]{:S(2)}) copy-start(bf16[3072,256]{1,0:T(8,128)(2,1)S(1)} %get-tuple-element.211) | copy-start | bytes 4718596
  209.9 12.4 %slice-start.4 = ((s8[18874368]{0:T(1024)(128)(4,1)}), s8[4194304]{0:T(1024)(128)(4,1)S(1)}, s32[]{:S(2)}) async-start(s8[18874368]{0:T(1024)(128)(4,1)} %bitcast.518), calls=%async_computation.21 | async-start | bytes 8388608
  244.0 90.5 %copy-start.11 = (f32[128,768]{1,0:T(8,128)}, f32[128,768]{1,0:T(8,128)S(1)}, u32[]{:S(2)}) copy-start(f32[128,768]{1,0:T(8,128)S(1)} %get-tuple-element.191) | copy-start | bytes 1179652
  323.6 207.5 %reduce-scatter.25.cloned.1.call-start = ((), (), s32[]{:S(2)}) async-start(), calls=%async_computation.14 | async-start | bytes 3981312
  378.5 13.5 %copy-start.14 = (bf16[512,3072]{1,0:T(8,128)(2,1)}, bf16[512,3072]{1,0:T(8,128)(2,1)S(1)}, u32[]{:S(2)}) copy-start(bf16[512,3072]{1,0:T(8,128)(2,1)S(1)} %get-tuple-element.224) | copy-start | bytes 9437188
  378.6 13.5 %copy-start.15 = (bf16[512,3072]{1,0:T(8,128)(2,1)}, bf16[512,3072]{1,0:T(8,128)(2,1)S(1)}, u32[]{:S(2)}) copy-start(bf16[512,3072]{1,0:T(8,128)(2,1)S(1)} %get-tuple-element.225) | copy-start | bytes 9437188
  378.6 13.5 %copy-start.136 = (f32[512]{0:T(512)S(1)}, f32[512]{0:T(512)}, u32[]{:S(2)}) copy-start(f32[512]{0:T(512)} %get-tuple-element.347) | copy-start | bytes 6148
  435.9 97.4 %reduce-scatter.15.cloned.1.call-start = ((), (), s32[]{:S(2)}) async-start(), calls=%async_computation.9 | async-start | bytes 1327104 | tf_op jit(solution)/shard_map/reduce_scatter | solution.py:330
  441.8 124.4 %reduce-scatter.13.cloned.1.call-start = ((), (), s32[]{:S(2)}) async-start(), calls=%async_computation.8 | async-start | bytes 1327104 | tf_op jit(solution)/shard_map/reduce_scatter | solution.py:330
  446.5 177.5 %reduce-scatter.23.cloned.1.call-start = ((), (), s32[]{:S(2)}) async-start(), calls=%async_computation.13 | async-start | bytes 5308416 | tf_op jit(solution)/shard_map/reduce_scatter | solution.py:345
  460.3 221.3 %reduce-scatter.21.cloned.1.call-start = ((), (), s32[]{:S(2)}) async-start(), calls=%async_computation.12 | async-start | bytes 5308416 | tf_op jit(solution)/shard_map/reduce_scatter | solution.py:345
  470.0 291.6 %reduce-scatter.19.cloned.1.call-start = ((), (), s32[]{:S(2)}) async-start(), calls=%async_computation.11 | async-start | bytes 10616832 | tf_op jit(solution)/shard_map/reduce_scatter | solution.py:342
  470.3 14.9 %copy-start.86 = (bf16[128,3072]{1,0:T(8,128)(2,1)S(1)}, bf16[128,3072]{1,0:T(8,128)(2,1)}, u32[]{:S(2)}) copy-start(bf16[128,3072]{1,0:T(8,128)(2,1)} %copy-done.85) | copy-start | bytes 2359300
  470.3 14.9 %copy-start.88 = (bf16[128,3072]{1,0:T(8,128)(2,1)S(1)}, bf16[128,3072]{1,0:T(8,128)(2,1)}, u32[]{:S(2)}) copy-start(bf16[128,3072]{1,0:T(8,128)(2,1)} %copy-done.87) | copy-start | bytes 2359300
  496.0 15.4 %copy-start.92 = (bf16[128,3072]{1,0:T(8,128)(2,1)S(1)}, bf16[128,3072]{1,0:T(8,128)(2,1)}, u32[]{:S(2)}) copy-start(bf16[128,3072]{1,0:T(8,128)(2,1)} %copy-done.91) | copy-start | bytes 2359300
  496.0 15.4 %copy-start.94 = (bf16[128,3072]{1,0:T(8,128)(2,1)S(1)}, bf16[128,3072]{1,0:T(8,128)(2,1)}, u32[]{:S(2)}) copy-start(bf16[128,3072]{1,0:T(8,128)(2,1)} %copy-done.93) | copy-start | bytes 2359300
  496.0 345.6 %reduce-scatter.17.cloned.1.call-start = ((), (), s32[]{:S(2)}) async-start(), calls=%async_computation.10 | async-start | bytes 10616832 | tf_op jit(solution)/shard_map/reduce_scatter | solution.py:342
  522.6 507.6 %all-reduce.22.cloned.1.call-start = ((), (), s32[]{:S(2)}) async-start(), calls=%async_computation.16 | async-start | bytes 10027008 | tf_op jit(solution)/shard_map/psum | solution.py:373
  531.1 323.0 %copy-start.127 = (f32[768]{0:T(1024)S(1)}, f32[768]{0:T(1024)}, u32[]{:S(2)}) copy-start(f32[768]{0:T(1024)} %get-tuple-element.116) | copy-start | bytes 9220
  531.1 323.0 %copy-start.128 = (f32[768]{0:T(1024)S(1)}, f32[768]{0:T(1024)}, u32[]{:S(2)}) copy-start(f32[768]{0:T(1024)} %get-tuple-element.133) | copy-start | bytes 9220
  531.1 323.0 %copy-start.129 = (f32[768]{0:T(1024)S(1)}, f32[768]{0:T(1024)}, u32[]{:S(2)}) copy-start(f32[768]{0:T(1024)} %get-tuple-element.108) | copy-start | bytes 9220
  531.1 323.0 %copy-start.130 = (f32[768]{0:T(1024)S(1)}, f32[768]{0:T(1024)}, u32[]{:S(2)}) copy-start(f32[768]{0:T(1024)} %get-tuple-element.125) | copy-start | bytes 9220
  531.1 389.1 %copy-start.47 = (bf16[768,768]{1,0:T(8,128)(2,1)S(1)}, bf16[768,768]{1,0:T(8,128)(2,1)}, u32[]{:S(2)}) copy-start(bf16[768,768]{1,0:T(8,128)(2,1)} %get-tuple-element.218) | copy-start | bytes 3538948
  531.1 389.1 %copy-start.75 = (bf16[12,64,128]{2,1,0:T(8,128)(2,1)S(1)}, bf16[12,64,128]{2,1,0:T(8,128)(2,1)}, u32[]{:S(2)}) copy-start(bf16[12,64,128]{2,1,0:T(8,128)(2,1)} %get-tuple-element.323) | copy-start | bytes 589828
  531.1 389.0 %copy-start.79 = (bf16[12,64,128]{2,1,0:T(8,128)(2,1)S(1)}, bf16[12,64,128]{2,1,0:T(8,128)(2,1)}, u32[]{:S(2)}) copy-start(bf16[12,64,128]{2,1,0:T(8,128)(2,1)} %fusion.92) | copy-start | bytes 589828
  (148 other events, 650.3 us)
Sparse Core Ops, SparseCore 0:
  323.7 48.4 reduce-scatter.26
  436.0 48.7 reduce-scatter.24
  488.6 36.7 reduce-scatter.14
  529.4 36.7 reduce-scatter.12
  570.1 53.8 reduce-scatter.22
  627.7 53.8 reduce-scatter.20
  685.1 76.4 reduce-scatter.18
  765.1 76.4 reduce-scatter.16
  845.7 184.4 all-reduce.21

commit v2 on v1

--- a/solution.py
+++ b/solution.py
@@ -1,4 +1,5 @@
 import functools
+import heapq
 import math
 
 import jax
@@ -907,78 +908,545 @@
     )(short_len, long_len, head_slopes(HEADS), w_qkv, w_out, w_gu, w_dn, packed, short_in, long_in)
 
 
-def backward_layer(l, state, lengths, valid, grad_rows_in, rows_of):
-    s = {name: value[l][rows_of] if name != "act" and name not in ("da", "db", "inner") else value[l][:, rows_of] for name, value in state["rows"].items()}
-    wq, wo, wg, wd = (state["w"][n][l] for n in ("qkv", "out", "gu", "dn"))
-    cat = lambda w: jnp.concatenate([w[i] for i in range(w.shape[0])], axis=1)
-    w_qkv, w_out, w_gu, w_dn = cat(wq), cat(wo), cat(wg), cat(wd)
-    vec = state["vec"][l * 8 : l * 8 + 8]
-    gain_one, gain_two = vec[3], vec[6]
-    row_count = grad_rows_in.shape[0]
-    cat2 = lambda a: jnp.concatenate([a[i] for i in range(a.shape[0])], axis=1)
-    da, db, inner = cat2(s["da"]), cat2(s["db"]), cat2(s["inner"])
-    score_scale = 0.125
-    gn = grad_rows_in * valid
-    grad_u, gaintwo, biastwo = normalize_back(gn, s["uhat"], s["r2"][:, :1], gain_two)
-    gd = grad_u.astype(jnp.bfloat16)
-    bdown = jnp.sum(gd, axis=0, dtype=jnp.float32)
-    wdown = rows_product(inner, gd)
-    gi = times_transpose(gd, w_dn)
-    ggu = jnp.concatenate([gi * da.astype(jnp.float32), gi * db.astype(jnp.float32)], axis=1).astype(jnp.bfloat16)
-    wgu = rows_product(s["hid"], ggu)
-    gh = grad_u + times_transpose(ggu, w_gu)
-    gv, gainone, biasone = normalize_back(gh, s["vhat"], s["r1"][:, :1], gain_one)
-    gb = gv.astype(jnp.bfloat16)
-    bout = jnp.sum(gb, axis=0, dtype=jnp.float32)
-    wout = rows_product(s["mixed"], gb)
-    gm = times_transpose(gb, w_out).astype(jnp.bfloat16)
-    n = row_count
-    q, k, v = (split_heads(s["act"][i], 1, n) for i in range(3))
-    gmh = split_heads(gm, 1, n)
-    pos = jnp.arange(n)
-    dist = jnp.abs(pos[:, None] - pos[None, :]).astype(jnp.float32)
-    sc = jnp.einsum("sqhd,skhd->shqk", q, k, preferred_element_type=jnp.float32) * score_scale
-    sc = sc - head_slopes(HEADS)[None, :, None, None] * dist[None, None]
-    sc = jnp.where((pos[None, :] < lengths[:, None])[:, None, None, :], sc, masked_score)
-    probs = jnp.exp(sc - s["lse"][:, :HEADS].T[None, :, :, None])
-    pl_ = probs.astype(jnp.bfloat16)
-    gp = jnp.einsum("sqhd,skhd->shqk", gmh, v, preferred_element_type=jnp.float32)
-    gs = (probs * (gp - jnp.sum(probs * gp, axis=-1, keepdims=True))).astype(jnp.bfloat16)
-    gq = (jnp.einsum("shqk,skhd->sqhd", gs, k, preferred_element_type=jnp.float32) * score_scale).astype(jnp.bfloat16).reshape(n, -1)
-    gk = (jnp.einsum("shqk,sqhd->skhd", gs, q, preferred_element_type=jnp.float32) * score_scale).astype(jnp.bfloat16).reshape(n, -1)
-    gvv = jnp.einsum("shqk,sqhd->skhd", pl_, gmh, preferred_element_type=jnp.float32).astype(jnp.bfloat16).reshape(n, -1)
-    gp3 = jnp.concatenate([gq, gk, gvv], axis=1)
-    wqkv = rows_product(s["x"], gp3)
-    gx = gv + times_transpose(gp3, w_qkv)
-    terms = (wqkv, jnp.sum(gq, axis=0, dtype=jnp.float32), jnp.sum(gvv, axis=0, dtype=jnp.float32), wout, bout, gainone, biasone, wgu, wdown, bdown, gaintwo, biastwo)
-    return gx, terms
+SLOTS = 6
+GRAD_SLOTS = 3
+GRADS = [("dn", 0), ("dn", 1), ("dn", 2), ("gu", 0), ("gu", 3), ("gu", 1), ("gu", 4), ("gu", 2), ("gu", 5)]
+GRADS += [("out", 0), ("qkv", 0), ("qkv", 1), ("qkv", 2)]
+GRAD_ROWS = {"dn": 768, "gu": 768, "out": 576, "qkv": 576}
+
+
+class Flow:
+    def __init__(self):
+        self.queue = []
+        self.added = 0
+        self.over = set()
+        self.clock = 0.0
+
+    def add(self, ready, name, act):
+        heapq.heappush(self.queue, (ready, self.added, name, act))
+        self.added += 1
+
+    def one(self):
+        ready, _, name, act = heapq.heappop(self.queue)
+        self.clock = max(self.clock, ready)
+        act()
+        self.over.add(name)
+
+    def step(self, cost):
+        self.clock += cost
+        while self.queue and self.queue[0][0] <= self.clock:
+            self.one()
+
+    def need(self, name):
+        while name not in self.over:
+            self.one()
+
+    def rest(self):
+        while self.queue:
+            self.one()
+
+
+def norm_back(grad, gain, normed, inverse):
+    scaled = grad * gain
+    return inverse * (
+        scaled
+        - jnp.mean(scaled, axis=1, keepdims=True)
+        - normed * jnp.mean(scaled * normed, axis=1, keepdims=True)
+    )
+
+
+def attend_back(act, grad_mixed, lse_t, dist, slopes, out, pair, base, size, place):
+    lane = lax.broadcasted_iota(jnp.int32, (1, 128), 1)
+    rows = pl.ds(base, size)
+    cols = pl.ds(pl.multiple_of(pair * 128, 128), 128)
+    q2, k2, v2, g2 = act[0, rows, cols], act[1, rows, cols], act[2, rows, cols], grad_mixed[rows, cols]
+    parts = []
+    for half in range(2):
+        head = 2 * pair + half
+        mine = (lane < 64) == (half == 0)
+        q_head = jnp.where(mine, q2, jnp.zeros_like(q2)) * jnp.bfloat16(0.125)
+        g_head = jnp.where(mine, g2, jnp.zeros_like(g2))
+        scores = mm(k2, q_head, NT) - slopes[head] * dist[...]
+        probs = jnp.exp(scores - lse_t[pl.ds(head, 1), rows])
+        grad_probs = mm(v2, g_head, NT)
+        dots = jnp.sum(probs * grad_probs, axis=0, keepdims=True)
+        grad_scores = (probs * (grad_probs - dots)).astype(jnp.bfloat16)
+        parts.append((
+            mm(grad_scores, k2, TN) * 0.125,
+            mm(grad_scores, q2, NN) * 0.125,
+            mm(probs.astype(jnp.bfloat16), g2, NN),
+        ))
+    for part in range(3):
+        out[part, rows, place] = jnp.where(lane < 64, parts[0][part], parts[1][part]).astype(jnp.bfloat16)
+
+
+def backward_kernel(
+    short_len, long_len, slopes,
+    k_qkv, k_out, k_gu, k_dn, k_vec, k_x1, k_act, k_mixed, k_lse, k_vhat, k_r1, k_hid, k_da, k_db, k_inner,
+    k_uhat, k_r2, x_short, x_long, cot_short, cot_long,
+    grad_short, grad_long, o_grads, o_vecs,
+    w_tall, w_gu, w_out, inner, da, db, work, normed, r_st, grad, total, low, rows_in, rows_t, mixed, act, gm,
+    dist_l, dist_s, lse, lse_t, vec, vecs, vec_in, own, got, got_x, got_y, both, got_z, got_w, fin,
+    load_sem, c_s, c_r, x_s, x_r, y_s, y_r, x2_s, x2_r, y2_s, y2_r, z_s, z_r, w_s, w_r, f_s, f_r, out_sem, v_s, v_r,
+):
+    long_rows, short_rows = dist_l.shape[0], dist_s.shape[0]
+    rows, width = grad.shape
+    me, z = lax.axis_index("zero"), lax.axis_index("dp")
+    c, x, y = lax.rem(me, 2), lax.rem(lax.div(me, 2), 2), lax.div(me, 4)
+    hz = lax.rem(z, 2)
+    to_c, to_x, to_y = (z, flip(me, 1)), (z, flip(me, 2)), (z, flip(me, 4))
+    to_z, to_w = (flip(z, 1), me), (flip(z, 2), me)
+
+    loads = {}
+    load_count = [0]
+
+    def load(name, pairs):
+        copies = []
+        for src, dst in pairs:
+            copies.append(pltpu.make_async_copy(src, dst, load_sem.at[load_count[0]]))
+            load_count[0] += 1
+        for copy in copies:
+            copy.start()
+        loads[name] = copies
+
+    def loaded(name):
+        for copy in loads.pop(name, []):
+            copy.wait()
+
+    def load_dn(l):
+        load("dn", [(k_dn.at[l, b], w_tall.at[:, pl.ds(256 * b, 256)]) for b in range(3)])
+
+    def load_qkv(l):
+        load("qkv", [(k_qkv.at[l, b], w_tall.at[pl.ds(width * b, width)]) for b in range(3)])
+
+    def load_x(l):
+        if l:
+            load("x", [(k_x1, rows_in)])
+        else:
+            load("x", [(x_long.at[0], rows_in.at[pl.ds(0, long_rows)]),
+                       (x_short.at[0], rows_in.at[pl.ds(long_rows, short_rows)])])
+
+    def load_gelu(l, b):
+        load("gelu", [(k_da.at[l, b], da), (k_db.at[l, b], db)])
+
+    top = LAYERS - 1
+    load("cot", [(cot_long.at[0], low.at[pl.ds(0, long_rows)]), (cot_short.at[0], low.at[pl.ds(long_rows, short_rows)])])
+    load("vec", [(k_vec, vec)])
+    load("uhat", [(k_uhat.at[top], normed), (k_r2.at[top], r_st)])
+    load("inner", [(k_inner.at[top], inner)])
+    load_dn(top)
+    load_gelu(top, 0)
+    load("hid", [(k_hid.at[top], rows_in)])
+    load("gu", [(k_gu.at[top], w_gu)])
+    load("out", [(k_out.at[top, 0], w_out)])
+    load("mixed", [(k_mixed.at[top], mixed)])
+    load("act", [(k_act.at[top], act), (k_lse.at[top], lse)])
+
+    barrier = pltpu.get_barrier_semaphore()
+    for partner in (to_c, to_x, to_y, to_z, to_w):
+        pl.semaphore_signal(barrier, inc=1, device_id=partner, device_id_type=MESH)
+    pl.semaphore_wait(barrier, 5)
+
+    flow = Flow()
+    chunks = [(l, kind, b) for l in reversed(range(LAYERS)) for kind, b in GRADS]
+    last = 8
+    free = {"x": 0.0, "y": 0.0, "z": 0.0}
+
+    def far(src, dst, send_sem, recv_sem, partner):
+        return pltpu.make_async_remote_copy(
+            src_ref=src, dst_ref=dst, send_sem=send_sem, recv_sem=recv_sem, device_id=partner, device_id_type=MESH
+        )
+
+    def plus(left, right):
+        return (left.astype(jnp.float32) + right.astype(jnp.float32)).astype(jnp.bfloat16)
+
+    class Chunk:
+        def __init__(self, n):
+            self.n = n
+            self.count = GRAD_ROWS[chunks[n][1]]
+            s, d, r, h = n % SLOTS, n % GRAD_SLOTS, self.count, self.count // 2
+            self.s, self.d, self.h = s, d, h
+            self.low, self.high, self.all = pl.ds(0, h), pl.ds(h, h), pl.ds(0, r)
+            self.c = far(own.at[d, :, :, 1 - c, self.all], got.at[s, :, :, self.all], c_s.at[s], c_r.at[s], to_c)
+            self.x = far(got.at[s, :, 1 - x, self.low], got_x.at[s, :, self.low], x_s.at[s], x_r.at[s], to_x)
+            self.y = far(got.at[s, 1 - y, :, self.high], got_y.at[s, :, self.low], y_s.at[s], y_r.at[s], to_y)
+            self.y2 = far(got_x.at[s, 1 - y, self.low], both.at[s, 0, self.low], y2_s.at[s], y2_r.at[s], to_y)
+            self.x2 = far(got_y.at[s, 1 - x, self.low], both.at[s, 1, self.low], x2_s.at[s], x2_r.at[s], to_x)
+            self.z = far(both.at[s, 1 - hz, self.low], got_z.at[s, self.low], z_s.at[s], z_r.at[s], to_z)
+            self.w = far(got_z.at[s, self.low], got_w.at[s, self.low], w_s.at[s], w_r.at[s], to_w)
+            self.f = far(fin.at[s, hz, self.low], fin.at[s, hz, self.low], f_s.at[s], f_r.at[s], to_z)
+            self.o = [
+                pltpu.make_async_copy(fin.at[s, i, self.low], o_grads.at[n, pl.ds(i * h, h)], out_sem.at[s, i])
+                for i in range(2)
+            ]
+
+        def run(self, stage):
+            n = self.n
+            if n + 2 - SLOTS >= 0:
+                flow.need((min(stage + 3, last), n + 2 - SLOTS))
+            if n >= 2:
+                flow.need((min(stage + 1, last), n - 2))
+            getattr(self, "stage%d" % stage)()
+
+        def later(self, stage, ready):
+            flow.add(ready, (stage, self.n), functools.partial(self.run, stage))
+
+        def lane(self, name, blocks, scale=1.0):
+            start = max(free[name], flow.clock)
+            free[name] = start + blocks * self.h * 256 / LINK_BYTES_PER_US * scale
+            return free[name] + 1.5
+
+        def emit(self):
+            self.run(1)
+            flow.over.add((1, self.n))
+
+        def stage1(self):
+            self.c.start()
+            self.later(2, flow.clock + 3.5)
+
+        def stage2(self):
+            self.c.wait()
+            for i in range(2):
+                for j in range(2):
+                    got[self.s, i, j, self.all] = plus(got[self.s, i, j, self.all], own[self.d, i, j, c, self.all])
+            self.x.start()
+            self.y.start()
+            self.later(3, max(self.lane("x", 2), self.lane("y", 2)))
+
+        def stage3(self):
+            self.x.wait_recv()
+            for i in range(2):
+                got_x[self.s, i, self.low] = plus(got_x[self.s, i, self.low], got[self.s, i, x, self.low])
+            self.y2.start()
+            self.y.wait_recv()
+            for i in range(2):
+                got_y[self.s, i, self.low] = plus(got_y[self.s, i, self.low], got[self.s, y, i, self.high])
+            self.x2.start()
+            self.later(4, max(self.lane("x", 1), self.lane("y", 1)))
+
+        def stage4(self):
+            self.y2.wait_recv()
+            both[self.s, 0, self.low] = plus(both[self.s, 0, self.low], got_x[self.s, y, self.low])
+            self.x2.wait_recv()
+            both[self.s, 1, self.low] = plus(both[self.s, 1, self.low], got_y[self.s, x, self.low])
+            self.z.start()
+            self.x.wait_send()
+            self.y.wait_send()
+            self.later(5, self.lane("z", 1))
+
+        def stage5(self):
+            self.z.wait_recv()
+            got_z[self.s, self.low] = plus(got_z[self.s, self.low], both[self.s, hz, self.low])
+            self.w.start()
+            self.y2.wait_send()
+            self.x2.wait_send()
+            self.later(6, self.lane("z", 1, 2.0))
+
+        def stage6(self):
+            self.w.wait_recv()
+            fin[self.s, hz, self.low] = plus(got_w[self.s, self.low], got_z[self.s, self.low])
+            self.f.start()
+            self.z.wait_send()
+            self.later(7, self.lane("z", 1))
+
+        def stage7(self):
+            self.f.wait()
+            self.w.wait_send()
+            for copy in self.o:
+                copy.start()
+            self.later(8, flow.clock + 2.0)
+
+        def stage8(self):
+            for copy in self.o:
+                copy.wait()
+
+    made = []
+
+    def room():
+        n = len(made)
+        if n >= GRAD_SLOTS:
+            flow.need((2, n - GRAD_SLOTS))
+        return n % GRAD_SLOTS
+
+    def emit():
+        made.append(Chunk(len(made)))
+        made[-1].emit()
+
+    def store(slot, block, product, per_owner):
+        wide = product.shape[1] // 128
+        for owner in range(8):
+            for b in range(wide):
+                own[slot, owner // 4, owner // 2 % 2, owner % 2, pl.ds((block + b) * per_owner, per_owner)] = product[
+                    owner * per_owner : (owner + 1) * per_owner, b * 128 : (b + 1) * 128
+                ].astype(jnp.bfloat16)
+
+    def vector(l, number):
+        return vec[pl.ds(l * 8 + number, 1), :]
+
+    def put(l, number, value):
+        vecs[pl.ds(l * 8 + number, 1), :] = value
+
+    def gather_put(l, number, value):
+        at = pl.ds(l * 8 + number, 1)
+        vecs[at, :] = vecs[at, :] + value
+
+    position = lax.broadcasted_iota(jnp.int32, (long_rows, long_rows), 0)
+    other = lax.broadcasted_iota(jnp.int32, (long_rows, long_rows), 1)
+    dist_l[...] = jnp.where(position < long_len[0], jnp.abs(position - other).astype(jnp.float32), 1e18)
+    position = lax.broadcasted_iota(jnp.int32, (short_rows, short_rows), 0)
+    other = lax.broadcasted_iota(jnp.int32, (short_rows, short_rows), 1)
+    dist_s[...] = jnp.where(position < short_len[0], jnp.abs(position - other).astype(jnp.float32), 1e18)
+    vecs[...] = jnp.zeros_like(vecs)
+    loaded("cot")
+    loaded("vec")
+    grad[...] = low[...].astype(jnp.float32)
+
+    for l in reversed(range(LAYERS)):
+        loaded("uhat")
+
+        def second_norm(r0):
+            part = pl.ds(r0, 128)
+            place = lax.broadcasted_iota(jnp.int32, (128, 1), 0) + r0
+            limit = jnp.where(place < long_rows, long_len[0], short_len[0] + long_rows)
+            g = jnp.where(place < limit, grad[part, :], 0.0)
+            unit = normed[part, :]
+            back = norm_back(g, vector(l, 6), unit, r_st[part, :1])
+            rounded = back.astype(jnp.bfloat16)
+            total[part, :] = back
+            low[part, :] = rounded
+            gather_put(l, 5, jnp.sum(rounded.astype(jnp.float32), axis=0, keepdims=True))
+            gather_put(l, 6, jnp.sum(g * unit, axis=0, keepdims=True))
+            gather_put(l, 7, jnp.sum(g, axis=0, keepdims=True))
+
+        row_loop(rows, 128, second_norm)
+        load("vhat", [(k_vhat.at[l], normed), (k_r1.at[l], r_st)])
+        flow.step(2.5)
+
+        loaded("inner")
+        span = inner.shape[2]
+        each = 3 * span // 8
+        piece = each // 3
+        for b in range(3):
+            slot = room()
+            columns = []
+            for owner in range(8):
+                first = owner * each + b * piece
+                columns.append(inner[first // span, :, pl.ds(first % span, piece)])
+            left = jnp.concatenate(columns, axis=1)
+            for j in range(3):
+                product = mm(left, low[:, pl.ds(j * 256, 256)], TN)
+                store(slot, 2 * j, product, piece)
+            emit()
+            flow.step(3.0)
+        if l:
+            load("inner", [(k_inner.at[l - 1], inner)])
+
+        loaded("hid")
+        rows_t[...] = rows_in[...].T
+        load_x(l)
+        loaded("dn")
+        loaded("gu")
+        half = w_gu.shape[0] // 2
+        for b in range(half):
+            loaded("gelu")
+
+            def inner_back(j, carry):
+                cols = pl.ds(pl.multiple_of(j * 256, 256), 256)
+                back = mm(low[...], w_tall[pl.ds(pl.multiple_of(b * span + j * 256, 256), 256), :], NT)
+                work[0, :, cols] = (back * da[:, cols].astype(jnp.float32)).astype(jnp.bfloat16)
+                work[1, :, cols] = (back * db[:, cols].astype(jnp.float32)).astype(jnp.bfloat16)
+                return carry
+
+            lax.fori_loop(0, span // 256, inner_back, 0)
+            if b < half - 1:
+                load_gelu(l, b + 1)
+            elif l:
+                load_gelu(l - 1, 0)
+            flow.step(2.0)
+            for side in range(2):
+                slot = room()
+
+                def weight_block(j, carry):
+                    cols = pl.ds(pl.multiple_of(j * 256, 256), 256)
+                    store(slot, 2 * j, mm(rows_t[...], work[side, :, cols], NN), width // 8)
+                    return carry
+
+                lax.fori_loop(0, span // 256, weight_block, 0)
+                emit()
+                flow.step(2.0)
+                total[...] += mm(work[side], w_gu[side * half + b], NT)
+                flow.step(2.0)
+        load_qkv(l)
+        if l:
+            load("gu", [(k_gu.at[l - 1], w_gu)])
+
+        loaded("vhat")
+
+        def first_norm(r0):
+            part = pl.ds(r0, 128)
+            g = total[part, :]
+            unit = normed[part, :]
+            back = norm_back(g, vector(l, 3), unit, r_st[part, :1])
+            rounded = back.astype(jnp.bfloat16)
+            grad[part, :] = back
+            low[part, :] = rounded
+            gather_put(l, 2, jnp.sum(rounded.astype(jnp.float32), axis=0, keepdims=True))
+            gather_put(l, 3, jnp.sum(g * unit, axis=0, keepdims=True))
+            gather_put(l, 4, jnp.sum(g, axis=0, keepdims=True))
+
+        row_loop(rows, 128, first_norm)
+        if l:
+            load("uhat", [(k_uhat.at[l - 1], normed), (k_r2.at[l - 1], r_st)])
+        flow.step(2.5)
+        loaded("out")
+        gm[...] = mm(low[...], w_out[...], NT).astype(jnp.bfloat16)
+        if l:
+            load("out", [(k_out.at[l - 1, 0], w_out)])
+        loaded("mixed")
+        slot = room()
+        for j in range(3):
+            store(slot, 2 * j, mm(mixed[...], low[:, pl.ds(j * 256, 256)], TN), width // 8)
+        emit()
+        if l:
+            load("mixed", [(k_mixed.at[l - 1], mixed)])
+        flow.step(3.0)
+
+        loaded("x")
+        rows_t[...] = rows_in[...].T
+        if l:
+            load("hid", [(k_hid.at[l - 1], rows_in)])
+        loaded("act")
+        lse_t[...] = lse[...].T
+        for group in range(3):
+            for step in range(2):
+                pair = 2 * group + step
+                place = pl.ds(pair * 128, 128)
+                attend_back(act, gm, lse_t, dist_l, slopes, work, pair, 0, long_rows, place)
+                attend_back(act, gm, lse_t, dist_s, slopes, work, pair, long_rows, short_rows, place)
+                flow.step(4.5)
+            slot = room()
+            for part in range(3):
+                store(slot, 2 * part, mm(rows_t[...], work[part, :, pl.ds(group * 256, 256)], NN), width // 8)
+            emit()
+            flow.step(1.5)
+        if l:
+            load("act", [(k_act.at[l - 1], act), (k_lse.at[l - 1], lse)])
+        for part, number in ((0, 0), (2, 1)):
+            put(l, number, jnp.sum(work[part, :, pl.ds(0, width)].astype(jnp.float32), axis=0, keepdims=True))
+        if l == 0:
+            hops = [
+                far(vecs if i == 0 else vec_in.at[i - 1], vec_in.at[i], v_s.at[i], v_r.at[i], partner)
+                for i, partner in enumerate((to_c, to_x, to_y, to_z, to_w))
+            ]
+
+            def hop(i):
+                hops[i].wait()
+                vec_in[i] = vec_in[i] + (vecs[...] if i == 0 else vec_in[i - 1])
+                if i + 1 < len(hops):
+                    hops[i + 1].start()
+                    flow.add(flow.clock + 3.0, ("hop", i + 1), functools.partial(hop, i + 1))
+
+            hops[0].start()
+            flow.add(flow.clock + 3.0, ("hop", 0), functools.partial(hop, 0))
+        loaded("qkv")
+        for part in range(3):
+            grad[...] += mm(work[part, :, pl.ds(0, width)], w_tall[pl.ds(part * width, width), :], NT)
+            flow.step(1.5)
+        if l:
+            load_dn(l - 1)
+
+    load("out_l", [(grad.at[pl.ds(0, long_rows)], grad_long.at[0])])
+    load("out_s", [(grad.at[pl.ds(long_rows, short_rows)], grad_short.at[0])])
+    flow.rest()
+    load("out_v", [(vec_in.at[4], o_vecs)])
+    for name in ("out_l", "out_s", "out_v"):
+        loaded(name)
+
+
+def backward(short_len, long_len, kept, x_short, x_long, cot_short, cot_long):
+    low, full = jnp.bfloat16, jnp.float32
+    n_long, n_short, width = x_long.shape[1], x_short.shape[1], x_long.shape[2]
+    rows = n_long + n_short
+    count = LAYERS * len(GRADS)
+    span = 1024
+    out_shape = [
+        jax.ShapeDtypeStruct(x_short.shape, full),
+        jax.ShapeDtypeStruct(x_long.shape, full),
+        jax.ShapeDtypeStruct((count, 768, 128), low),
+        jax.ShapeDtypeStruct((16, width), full),
+    ]
+    vm = pltpu.VMEM
+    dma = pltpu.SemaphoreType.DMA
+    scratch = [
+        vm((3072, width), low), vm((6, width, span), low), vm((width, width), low),
+        vm((3, rows, span), low), vm((rows, span), low), vm((rows, span), low), vm((3, rows, span), low),
+        vm((rows, width), full), vm((rows, 128), full), vm((rows, width), full), vm((rows, width), full),
+        vm((rows, width), low), vm((rows, width), low), vm((width, rows), low), vm((rows, width), low),
+        vm((3, rows, width), low), vm((rows, width), low),
+        vm((n_long, n_long), full), vm((n_short, n_short), full), vm((rows, 128), full), vm((128, rows), full),
+        vm((16, width), full), vm((16, width), full), vm((5, 16, width), full),
+        vm((GRAD_SLOTS, 2, 2, 2, 768, 128), low), vm((SLOTS, 2, 2, 768, 128), low),
+        vm((SLOTS, 2, 384, 128), low), vm((SLOTS, 2, 384, 128), low), vm((SLOTS, 2, 384, 128), low),
+        vm((SLOTS, 384, 128), low), vm((SLOTS, 384, 128), low), vm((SLOTS, 2, 384, 128), low),
+    ]
+    scratch += [dma((96,))] + [dma((SLOTS,))] * 16 + [dma((SLOTS, 2)), dma((5,)), dma((5,))]
+    smem = pl.BlockSpec(memory_space=pltpu.SMEM)
+    hbm = pl.BlockSpec(memory_space=pl.ANY)
+    return pl.pallas_call(
+        backward_kernel,
+        out_shape=out_shape,
+        in_specs=[smem] * 3 + [hbm] * (len(kept) + 4),
+        out_specs=[hbm] * len(out_shape),
+        scratch_shapes=scratch,
+        compiler_params=pltpu.CompilerParams(
+            collective_id=1, has_side_effects=True, vmem_limit_bytes=VMEM_LIMIT
+        ),
+        cost_estimate=pl.CostEstimate(flops=60 * 10**9, bytes_accessed=2 * 10**8, transcendentals=10**7),
+    )(short_len, long_len, head_slopes(HEADS), *kept, x_short, x_long, cot_short, cot_long)
+
+
+def unpack(packed, vec_sums, shard):
+    found = {}
+    order = [(l, kind, b) for l in reversed(range(LAYERS)) for kind, b in GRADS]
+    for n, key in enumerate(order):
+        found[key] = packed[n]
+
+    def layer(l):
+        def columns(block, per_owner, count):
+            cut = block[: per_owner * count].reshape(count, per_owner, 128)
+            return jnp.swapaxes(cut, 0, 1)
+
+        gu = jnp.concatenate([columns(found[(l, "gu", b)], shard, 8) for b in range(6)], axis=1)
+        out = columns(found[(l, "out", 0)], shard, 6)
+        groups = [columns(found[(l, "qkv", b)], shard, 6).reshape(shard, 3, 256) for b in range(3)]
+        qkv = jnp.stack(groups, axis=2)
+        dn = jnp.concatenate([columns(found[(l, "dn", b)], 128, 6).reshape(128, 768) for b in range(3)], axis=0)
+        return (qkv.reshape(shard, -1), out.reshape(shard, -1), gu.reshape(shard, -1), dn)
+
+    layers = [layer(l) for l in range(LAYERS)]
+    weights = [jnp.stack([layers[l][i] for l in range(LAYERS)]).astype(jnp.float32) for i in range(4)]
+    mine = lax.dynamic_slice_in_dim(vec_sums, lax.axis_index("zero") * shard, shard, axis=1)
+    small = jnp.swapaxes(mine.reshape(LAYERS, 8, shard), 0, 1)
+    return weights, small
 
 
 def per_device_fused(
     short_in, long_in, short_lengths, long_lengths, w_qkv, q_bias, v_bias, w_out, out_bias, norm1_gain, norm1_bias,
     w_gate_up, w_down, down_bias, norm2_gain, norm2_bias, short_cot, long_cot,
 ):
-    params = (w_qkv, q_bias, v_bias, w_out, out_bias, norm1_gain, norm1_bias, w_gate_up, w_down, down_bias, norm2_gain, norm2_bias)
-    (short_out, long_out, k_qkv, k_out, k_gu, k_dn, vec, x1, act, mixed, lse, vhat, r1, hid, da, db, inner, uhat, r2) = forward(short_lengths, long_lengths, params, short_in, long_in)
-    x = jnp.stack([jnp.concatenate([long_in[0], short_in[0]]), x1])
-    state = {
-        "rows": dict(x=x, act=act, mixed=mixed, lse=lse, vhat=vhat, r1=r1, hid=hid, da=da, db=db, inner=inner, uhat=uhat, r2=r2),
-        "w": dict(qkv=k_qkv, out=k_out, gu=k_gu, dn=k_dn),
-        "vec": vec,
-    }
-    nl, ns = long_in.shape[1], short_in.shape[1]
-    grads = [long_cot[0].astype(jnp.float32), short_cot[0].astype(jnp.float32)]
-    spans = [slice(0, nl), slice(nl, nl + ns)]
-    lens = [long_lengths, short_lengths]
-    valids = [(jnp.arange(n) < le[0]).astype(jnp.float32)[:, None] for n, le in ((nl, long_lengths), (ns, short_lengths))]
-    reduced = [None] * LAYERS
-    for l in reversed(range(LAYERS)):
-        terms = [None, None]
-        for b in range(2):
-            grads[b], terms[b] = backward_layer(l, state, lens[b], valids[b], grads[b], spans[b])
-        reduced[l] = reduce_grads(jax.tree.map(jnp.add, *terms))
-    stacked = [jnp.stack([reduced[l][m] for l in range(LAYERS)]) for m in range(len(params))]
-    return (short_out, long_out, grads[1][None], grads[0][None]) + tuple(stacked)
+    params = (
+        w_qkv, q_bias, v_bias, w_out, out_bias, norm1_gain, norm1_bias, w_gate_up, w_down, down_bias,
+        norm2_gain, norm2_bias,
+    )
+    short_out, long_out, *kept = forward(short_lengths, long_lengths, params, short_in, long_in)
+    grad_short, grad_long, packed, vec_sums = backward(
+        short_lengths, long_lengths, kept, short_in, long_in, short_cot, long_cot
+    )
+    (g_qkv, g_out, g_gu, g_dn), small = unpack(packed, vec_sums, w_qkv.shape[1])
+    return (
+        short_out, long_out, grad_short, grad_long,
+        g_qkv, small[0], small[1], g_out, small[2], small[3], small[4], g_gu, g_dn, small[5], small[6], small[7],
+    )
 
 
 def solution(mesh):

time: 1050 us -> 410 us (0.39)
  waiting for transfers between devices: 411 us -> 0 us
  Pallas kernels: 155 us -> 374 us
  matrix products: 216 us -> 0 us
  local copies, waits for them, and re-layouts: 135 us -> 25.1 us
  other arithmetic: 72.5 us -> 5.49 us
  blocking collectives: 39.7 us -> 0 us
  between operations: 17.9 us -> 2.52 us
    reduce_scatter x6 -> x0, waiting for transfers between devices: 308 us -> none  [the longest x2 160 us: reduce_grads(): lax.psum_scatter(gateup_grad.astype(jnp.bfloat16), 'zero', scatter_dimens...]
    pallas_call x0 -> x1, Pallas kernels: none -> 219 us  [backward(): pl.pallas_call(backward_kernel, out_shape=out_shape, in_specs=[smem] * 3...]
    dot_general x52 -> x0, matrix products: 216 us -> none  [the longest x16 83.4 us: rows_product(): lax.dot_general(left, right, (((0,), (0,)), ((), ())), preferred_element_...]
    psum x1 -> x0, waiting for transfers between devices: 103 us -> none  [reduce_grads(): lax.psum(qkv_owned.astype(jnp.bfloat16), 'dp').astype(jnp.float32)]
    squeeze x15 -> x0, local copies, waits for them, and re-layouts: 38.9 us -> none  [the longest x10 16.8 us: backward_layer(): cat2 = lambda a: jnp.concatenate([a[i] for i in range(a.shape[0])], axis=1)]
    unnamed x361 -> x42, local copies, waits for them, and re-layouts: 43.7 us -> 10.8 us
    unnamed x1 -> x0, blocking collectives: 25.9 us -> none
    reduce_sum x10 -> x0, other arithmetic: 24.2 us -> none  [the longest x4 11.8 us: backward_layer(): bdown = jnp.sum(gd, axis=0, dtype=jnp.float32)]
  transfers between devices with their start and end apart: 9 -> 0, of which waited for: 6 -> 0; matrix products, arithmetic and copies ran while one was open for 23% -> 0% of each run, Pallas kernels for 0% -> 0%
where the time goes in v2:
time: 410 us; the launch traced here: 407 us
  Pallas kernels  374 us (91%)
  local copies, waits for them, and re-layouts  25.1 us (6%)
  other arithmetic  5.49 us (1%)
    pallas_call x1, Pallas kernels, backward(): pl.pallas_call(backward_kernel, out_shape=out_shape, in_specs=[smem] * 3...  219 us
    pallas_call x1, Pallas kernels, forward(): pl.pallas_call(forward_kernel, out_shape=out_shape, in_specs=[smem] * 3 +...  155 us
    unnamed x42, local copies, waits for them, and re-layouts  10.8 us

profile of v2, /device:TPU:0, one launch (start us, length us, event | category | flops | bytes accessed | tf_op | source)
XLA Modules:
  0.0 407.2 jit_solution(8653911713830041879)
XLA Ops:
  1.9 0.7 constant_dynamic-update-slice_fusion.7
  2.6 0.7 constant_dynamic-update-slice_fusion.6
  3.3 0.7 constant_dynamic-update-slice_fusion.5
  3.9 0.7 constant_dynamic-update-slice_fusion.4
  4.6 0.7 constant_dynamic-update-slice_fusion.3
  5.2 0.7 constant_dynamic-update-slice_fusion.2
  5.9 0.7 constant_dynamic-update-slice_fusion.1
  6.6 0.7 constant_dynamic-update-slice_fusion
  7.2 0.6 pad.4.vecs
  7.8 155.0 %shard_map.315 = (bf16[1,128,768]{2,1,0:T(8,128)(2,1)}, bf16[1,512,768]{2,1,0:T(8,128)(2,1)}, bf16[2,3,768,768]{3,2,1,0:T(8,128)(2,1)}, bf16[2,1,768,768]{3,2,1,...) custom-call(s32[1]{0:T(128)S(6)} %copy.94.short_len, ...), custom_call_target="tpu_custom_call" | custom-call | flops 25999998976 | bytes 200000000 | tf_op jit(solution)/shard_map/pallas_call | solution.py:898
  162.8 219.1 %shard_map.316 = (f32[1,128,768]{2,1,0:T(8,128)}, f32[1,512,768]{2,1,0:T(8,128)}, bf16[26,768,128]{2,1,0:T(8,128)(2,1)}, f32[16,768]{1,0:T(8,128)}) custom-call(s32[1]{0:T(128)S(6)} %copy.94.short_len, s32[1]{0:T(128)S(6)} %copy.95.long_len, f32[12]{0:T(128)} %constant.14.clone.slopes, bf16[2,3,768,768]{3,2,1,0:T(8,128)(2,1)} %get-tuple-element.41.k_qkv, ...), custom_call_target="tpu_custom_call" | custom-call | flops 60000002048 | bytes 200000000 | tf_op jit(solution)/shard_map/pallas_call | solution.py:1395
  381.9 1.4 fusion.1
  384.3 0.7 copy.55
  384.9 0.5 stack_reshape.43
  386.2 0.7 copy.51
  386.8 0.5 stack_reshape.39
  387.3 1.3 maximum_convert_fusion.2
  388.7 0.8 dynamic-slice_bitcast_fusion
  389.4 0.6 fusion.2
  390.6 0.9 maximum_convert_fusion.3
  391.4 3.2 fusion
  394.8 0.5 copy.59
  395.3 0.5 stack_reshape.47
  396.1 0.5 copy.58
  396.5 0.5 stack_reshape.46
  397.1 2.5 maximum_convert_fusion
  400.2 0.4 copy-done.3
  401.4 2.0 copy.66
  403.4 0.7 copy.96
  404.1 0.9 copy.97
  405.0 0.7 copy.98
  405.8 1.1 copy.99
  (52 shorter events, 3.9 us)
Async XLA Ops:
  397.1 2.5 copy-start.6
  397.1 2.7 copy-start.5
  397.1 2.9 copy-start.4
  399.6 0.9 copy-start.3
  399.6 1.1 copy-start.2
  399.6 1.3 copy-start.1
  401.4 2.0 copy-start.9
  401.4 2.6 copy-start.7
  403.4 1.6 copy-start.8
  404.1 1.7 copy-start
